TPU v7x, 32 devices: a whole 2x2x4 slice. The times are simulated.
32 devices in a mesh: seq: 16 (over z, y, x), ch: 2 (over core).
Axes of the slice: x: 2, y: 2, z: 4, core: 2. Of those that a mesh axis runs over, the one named last changes fastest.
Arguments:
- stream_one: bfloat16 [2048, 2048], P('seq', 'ch'), may hold values from -6 to 6
- stream_two: bfloat16 [2048, 2048], P('seq', 'ch'), may hold values from -6 to 6
- stream_value: bfloat16 [2048, 2048], P('seq', 'ch'), may hold values from -6 to 6
- long_filter: bfloat16 [2048, 2048], P('seq', 'ch'), may hold values from -4 to 4
- short_taps: float32 [3, 3, 2048], P(None, None, 'ch'), may hold values from -3.5 to 3.5
- skip_gain: float32 [2048], P('ch'), may hold values from -1 to 1
- out_grad: bfloat16 [2048, 2048], P('seq', 'ch'), may hold values from -0.59765625 to 0.59765625
Outputs:
- mixed_out: bfloat16 [2048, 2048], P('seq', 'ch')
- grad_one: bfloat16 [2048, 2048], P('seq', 'ch')
- grad_two: bfloat16 [2048, 2048], P('seq', 'ch')
- grad_value: bfloat16 [2048, 2048], P('seq', 'ch')
- grad_filter: float32 [2048, 2048], P('seq', 'ch')
- grad_taps: float32 [3, 3, 2048], P(None, None, 'ch')
- grad_skip: float32 [2048], P('ch')
All inputs are finite; a program needn't handle non-finite values.
Results may differ from a plain program's by a relative error of at most 0.0054.
Values may be sent and summed in bfloat16 or wider, within the bound.
No kernel may reach another device: no remote copies, remote signals or barrier semaphores. Data moves between devices by JAX's collectives and lax.ppermute only.
A program may use at most 128 MiB of HBM per device.

v0:
```python
import math

import jax
import jax.numpy as jnp
from jax import lax
from jax.sharding import PartitionSpec as P

exact_mode = lax.Precision.HIGHEST


def passed_along(block, axis, distance):
    devices = range(lax.axis_size(axis))
    route = [(i - distance, i) for i in devices if i - distance in devices]
    return lax.ppermute(block, axis, route)


def swapped(array, axis, apart):
    return lax.ppermute(array, axis, [(i, i ^ 1 << apart) for i in range(lax.axis_size(axis))])


def unit_root(exponent, modulus):
    reduced = jnp.mod(exponent, modulus).astype(jnp.float32)
    phases = reduced * jnp.float32(-2.0 * math.pi / modulus)
    return (jnp.cos(phases), jnp.sin(phases))


def reverse_bits(values, sections):
    result = jnp.zeros_like(values)
    for bit_pos in range(sections):
        result = result + jnp.bitwise_and(jnp.right_shift(values, bit_pos), 1) * (
            1 << sections - 1 - bit_pos
        )
    return result


def rotate_pair(values, cosine, sine_part):
    shape_rest = values.shape[1:]
    flipped = values.reshape((2, 2) + shape_rest)[:, ::-1].reshape(values.shape)
    signs = jnp.array([-1.0, 1.0, -1.0, 1.0], jnp.float32).reshape((4,) + (1,) * len(shape_rest))
    return values * cosine + flipped * (signs * sine_part)


def lift_raw(raw_vals, dev_index, doubled):
    cosine, sine_part = unit_root(dev_index, doubled)
    return jnp.stack([raw_vals, jnp.zeros_like(raw_vals), raw_vals * cosine, raw_vals * sine_part])


def upper_flag(dev_index, bit_pos):
    return jnp.bitwise_and(jnp.right_shift(dev_index, bit_pos), 1) == 1


def forward_section(current, partner_vals, dev_index, bit_pos):
    half_span = 1 << bit_pos
    is_upper = upper_flag(dev_index, bit_pos)
    cosine, sine_part = unit_root(jnp.mod(dev_index, half_span), 2 * half_span)
    return jnp.where(
        is_upper, rotate_pair(partner_vals - current, cosine, sine_part), current + partner_vals
    )


def inverse_section(current, partner_vals, dev_index, bit_pos):
    half_span = 1 << bit_pos
    is_upper = upper_flag(dev_index, bit_pos)
    cosine, sine_part = unit_root(jnp.mod(dev_index, half_span), 2 * half_span)
    return jnp.where(
        is_upper,
        partner_vals - rotate_pair(current, cosine, -sine_part),
        current + rotate_pair(partner_vals, cosine, -sine_part),
    )


def fold_parities(current, exponent, doubled):
    cosine, sine_part = unit_root(exponent, doubled)
    real_part = current[0] + current[2] * cosine - current[3] * sine_part
    imag_part = current[1] + current[2] * sine_part + current[3] * cosine
    return (real_part, imag_part)


def settle_terms(current, dev_index, partner_index, bit_pos, doubled):
    half_span = 1 << bit_pos
    is_upper = upper_flag(dev_index, bit_pos)
    cosine, sine_part = unit_root(jnp.mod(dev_index, half_span), 2 * half_span)
    own_real, own_imag = fold_parities(current, -dev_index, doubled)
    peer_real, peer_imag = fold_parities(current, -partner_index, doubled)
    kept_part = jnp.where(is_upper, -(cosine * own_real + sine_part * own_imag), own_real)
    sent_part = jnp.where(is_upper, cosine * peer_real + sine_part * peer_imag, peer_real)
    return (kept_part, sent_part)


def spectral_tables(freq_slot, tokens, doubled):
    modulus = doubled * tokens
    freq_rows = jnp.arange(tokens, dtype=jnp.int32)[:, None]
    place_cols = jnp.arange(tokens, dtype=jnp.int32)[None, :]
    forward_list = []
    inverse_list = []
    for parity in range(2):
        global_freq = doubled * freq_rows + 2 * freq_slot + parity
        cosine, sine_part = unit_root(global_freq * place_cols, modulus)
        forward_list.append(
            jnp.concatenate(
                [jnp.concatenate([cosine, -sine_part], 1), jnp.concatenate([sine_part, cosine], 1)],
                0,
            )
        )
        inverse_list.append(
            jnp.concatenate(
                [
                    jnp.concatenate([cosine.T, sine_part.T], 1),
                    jnp.concatenate([-sine_part.T, cosine.T], 1),
                ],
                0,
            )
        )
    return (jnp.stack(forward_list), jnp.stack(inverse_list))


def per_device(stream_one, stream_two, stream_value, long_filter, short_taps, skip_gain, out_grad):
    devices = lax.axis_size("seq")
    sections = devices.bit_length() - 1
    top_bit = sections - 1
    dev_index = lax.axis_index("seq")
    partner_index = jnp.bitwise_xor(dev_index, 1 << top_bit)
    tokens = stream_one.shape[0]
    channels = stream_one.shape[1]
    doubled = 2 * devices
    modulus = doubled * tokens
    tap_count = short_taps.shape[1]
    streams = jnp.stack([stream_one, stream_two, stream_value])
    before = passed_along(streams[:, tokens - (tap_count - 1) :], "seq", 1)
    extended = jnp.concatenate([before, streams], axis=1).astype(jnp.float32)
    convolved = jnp.zeros(streams.shape, jnp.float32)
    for offset in range(tap_count):
        first_row = tap_count - 1 - offset
        convolved = (
            convolved + short_taps[:, offset, None, :] * extended[:, first_row : first_row + tokens]
        )
    gate_out, gate_in, value_conv = (convolved[0], convolved[1], convolved[2])
    cotangent = out_grad.astype(jnp.float32)
    mixed_in = lax.optimization_barrier((gate_in * value_conv).astype(jnp.bfloat16))
    back_grad = lax.optimization_barrier((cotangent * gate_out).astype(jnp.bfloat16))
    mixed_wide = mixed_in.astype(jnp.float32)
    back_wide = back_grad.astype(jnp.float32)
    raw_stack = jnp.stack([mixed_in, back_grad, long_filter], axis=1)
    freq_slot = reverse_bits(dev_index, sections)
    partner_raw = swapped(raw_stack, "seq", top_bit)
    current = forward_section(
        lift_raw(raw_stack.astype(jnp.float32), dev_index, doubled),
        lift_raw(partner_raw.astype(jnp.float32), partner_index, doubled),
        dev_index,
        top_bit,
    )
    for bit_pos in range(top_bit - 1, -1, -1):
        partner_vals = swapped(current, "seq", bit_pos)
        current = forward_section(current, partner_vals, dev_index, bit_pos)
    spectrum = current
    forward_tab, inverse_tab = spectral_tables(freq_slot, tokens, doubled)
    packed = spectrum.reshape(2, 2 * tokens, 3 * channels)
    spectral = jnp.einsum(
        "rkb,rbx->rkx",
        forward_tab,
        packed,
        precision=exact_mode,
        preferred_element_type=jnp.float32,
    )
    spectral = spectral.reshape(2, 2, tokens, 3, channels)
    mix_real, mix_imag = (spectral[:, 0, :, 0], spectral[:, 1, :, 0])
    back_real, back_imag = (spectral[:, 0, :, 1], spectral[:, 1, :, 1])
    filt_real, filt_imag = (spectral[:, 0, :, 2], spectral[:, 1, :, 2])
    conv_spec = jnp.stack(
        [mix_real * filt_real - mix_imag * filt_imag, mix_real * filt_imag + mix_imag * filt_real],
        1,
    )
    grad_mix_spec = jnp.stack(
        [
            back_real * filt_real + back_imag * filt_imag,
            back_imag * filt_real - back_real * filt_imag,
        ],
        1,
    )
    grad_filt_spec = jnp.stack(
        [back_real * mix_real + back_imag * mix_imag, back_imag * mix_real - back_real * mix_imag],
        1,
    )
    products = jnp.stack([conv_spec, grad_mix_spec, grad_filt_spec], axis=3).reshape(
        2, 2 * tokens, 3 * channels
    )
    returned = jnp.einsum(
        "rbk,rkx->rbx",
        inverse_tab,
        products,
        precision=exact_mode,
        preferred_element_type=jnp.float32,
    )
    returned = returned.reshape(4, tokens, 3, channels)
    current = returned
    for bit_pos in range(top_bit):
        partner_vals = swapped(current, "seq", bit_pos)
        current = inverse_section(current, partner_vals, dev_index, bit_pos)
    kept_part, sent_part = settle_terms(current, dev_index, partner_index, top_bit, doubled)
    circular = (kept_part + swapped(sent_part, "seq", top_bit)) * jnp.float32(1.0 / modulus)
    long_out = circular[:, 0] + skip_gain * mixed_wide
    mixed_out = (gate_out * long_out).astype(jnp.bfloat16)
    grad_mixed_in = circular[:, 1] + skip_gain * back_wide
    grad_filter = circular[:, 2]
    grad_skip_local = jnp.sum(back_wide * mixed_wide, axis=0)
    conv_grads = jnp.stack(
        [cotangent * long_out, grad_mixed_in * value_conv, grad_mixed_in * gate_in]
    )
    taps_list = []
    for offset in range(tap_count):
        first_row = tap_count - 1 - offset
        taps_list.append(jnp.sum(conv_grads * extended[:, first_row : first_row + tokens], axis=1))
    grad_taps_local = jnp.stack(taps_list, axis=1)
    next_rows = passed_along(conv_grads[:, : tap_count - 1], "seq", -1)
    trailing = jnp.concatenate([conv_grads, next_rows], axis=1)
    grad_streams = jnp.zeros_like(conv_grads)
    for offset in range(tap_count):
        grad_streams = (
            grad_streams + short_taps[:, offset, None, :] * trailing[:, offset : offset + tokens]
        )
    grad_streams = grad_streams.astype(jnp.bfloat16)
    grad_taps, grad_skip = lax.psum((grad_taps_local, grad_skip_local), "seq")
    return (
        mixed_out,
        grad_streams[0],
        grad_streams[1],
        grad_streams[2],
        grad_filter,
        grad_taps,
        grad_skip,
    )


def solution(mesh):
    in_specs = (
        P("seq", "ch"),
        P("seq", "ch"),
        P("seq", "ch"),
        P("seq", "ch"),
        P(None, None, "ch"),
        P("ch"),
        P("seq", "ch"),
    )
    out_specs = (
        P("seq", "ch"),
        P("seq", "ch"),
        P("seq", "ch"),
        P("seq", "ch"),
        P("seq", "ch"),
        P(None, None, "ch"),
        P("ch"),
    )
    return jax.shard_map(
        per_device, mesh=mesh, in_specs=in_specs, out_specs=out_specs, check_vma=False
    )
```

profile of v0, /device:TPU:0, one launch (start us, length us, event | category | flops | bytes accessed | tf_op | source)
XLA Modules:
  0.0 1333.3 jit_solution(2861868372421501134)
XLA Ops:
  21.1 30.9 %collective-permute-done.1 = bf16[128,3,1024]{2,0,1:T(8,128)(2,1)} collective-permute-done((bf16[128,3,1024]{2,0,1:T(8,128)(2,1)}, bf16[128,3,1024]{2,0,1:T(8,128)(2,1)}, u32[]{:S(2)}, u32[]{:S(2)}) %collective-permute-start.1) | collective-permute-done | bytes 786464 | tf_op jit(solution)/shard_map/ppermute | solution.py:18
  65.5 7.5 fusion.22
  73.8 135.9 %collective-permute-done.2 = f32[4,128,3,1024]{3,1,2,0:T(8,128)} collective-permute-done((f32[4,128,3,1024]{3,1,2,0:T(8,128)}, f32[4,128,3,1024]{3,1,2,0:T(8,128)}, u32[]{:S(2)}, u32[]{:S(2)}) %collective-permute-start.2) | collective-permute-done | bytes 6291488 | tf_op jit(solution)/shard_map/ppermute | solution.py:18
  209.7 10.0 fusion.90
  226.2 15.3 %fusion.20 = f32[4,128,3,1024]{3,1,2,0:T(8,128)} fusion(f32[2,2,128,3,1024]{4,2,3,1,0:T(8,128)} %rev.31, f32[4,128,3,1024]{3,1,2,0:T(8,128)} %collective-permute-done.2, f32[4,128,3,1024]{3,1,2,0:T(8,128)} %fusion.90, f32[4]{0:T(128)S(1)} %get-tuple-element.66, f32[]{:T(128)S(6)} %cos.45, pred[]{:T(512)S(6)} %eq.41, f32[4]{0:T(128)S(1)} %get-tuple-element.67, ...), kind=kLoop, calls=%fused_computation.32 | loop fusion | flops 26738688 | bytes 40894520 | tf_op jit(solution)/shard_map/jit(_where)/select_n | solution.py:56
  242.3 135.5 %collective-permute-done.3 = f32[4,128,3,1024]{3,1,2,0:T(8,128)} collective-permute-done((f32[4,128,3,1024]{3,1,2,0:T(8,128)}, f32[4,128,3,1024]{3,1,2,0:T(8,128)}, u32[]{:S(2)}, u32[]{:S(2)}) %collective-permute-start.3) | collective-permute-done | bytes 6291488 | tf_op jit(solution)/shard_map/ppermute | solution.py:18
  377.8 9.4 sub.79
  393.7 14.8 %fusion.18 = f32[4,128,3,1024]{3,1,2,0:T(8,128)} fusion(f32[2,2,128,3,1024]{4,2,3,1,0:T(8,128)} %rev.32, f32[4,128,3,1024]{3,1,2,0:T(8,128)} %fusion.20, f32[4,128,3,1024]{3,1,2,0:T(8,128)} %collective-permute-done.3, f32[4,128,3,1024]{3,1,2,0:T(8,128)} %sub.79, f32[4]{0:T(128)S(1)} %get-tuple-element.65, f32[]{:T(128)S(6)} %cos.46, pred[]{:T(512)S(6)} %eq.42), kind=kLoop, calls=%fused_computation.29 | loop fusion | flops 7864320 | bytes 31457300 | tf_op jit(solution)/shard_map/jit(_where)/select_n | solution.py:56
  410.4 133.3 %collective-permute-done.4 = f32[4,128,3,1024]{3,1,2,0:T(8,128)} collective-permute-done((f32[4,128,3,1024]{3,1,2,0:T(8,128)}, f32[4,128,3,1024]{3,1,2,0:T(8,128)}, u32[]{:S(2)}, u32[]{:S(2)}) %collective-permute-start.4) | collective-permute-done | bytes 6291488 | tf_op jit(solution)/shard_map/ppermute | solution.py:18
  543.7 9.4 sub.80
  559.7 15.1 %fusion.16 = f32[4,128,3,1024]{3,1,2,0:T(8,128)} fusion(f32[4,128,3,1024]{3,1,2,0:T(8,128)} %sub.80, f32[2,2,128,3,1024]{4,2,3,1,0:T(8,128)} %rev.33, f32[4,128,3,1024]{3,1,2,0:T(8,128)} %fusion.18, f32[4,128,3,1024]{3,1,2,0:T(8,128)} %collective-permute-done.4, f32[4]{0:T(128)S(1)} %copy-done.27, pred[]{:T(512)S(6)} %eq.43), kind=kLoop, calls=%fused_computation.26 | loop fusion | flops 6291456 | bytes 31457296 | tf_op jit(solution)/shard_map/jit(_where)/select_n | solution.py:56
  574.8 10.4 copy.166
  585.2 11.4 reshape.514
  596.5 13.7 %fusion.44 = f32[2,256,3072]{1,2,0:T(8,128)} fusion(f32[2,256,3072]{2,1,0:T(8,128)} %reshape.514, f32[1,256,256]{2,1,0:T(8,128)S(1)} %maximum_bitcast_fusion.6, f32[1,256,256]{2,1,0:T(8,128)S(1)} %maximum_bitcast_fusion.5), kind=kOutput, calls=%fused_computation.98 | convolution fusion | flops 4831969280 | bytes 13107200 | tf_op jit(solution)/shard_map/rkb,rbx->rkx/dot_general | solution.py:158
  610.2 8.3 reshape.500
  618.5 11.9 fusion.86
  653.1 10.2 copy.155
  663.3 9.0 reshape.516
  672.4 18.0 %fusion.40 = f32[2,256,3072]{2,1,0:T(8,128)} fusion(f32[2,256,3072]{1,2,0:T(8,128)} %reshape.516, f32[1,256,256]{2,1,0:T(8,128)S(1)} %copy-done.16, f32[1,256,256]{2,1,0:T(8,128)S(1)} %maximum_bitcast_fusion.3), kind=kOutput, calls=%fused_computation.94 | convolution fusion | flops 4831969280 | bytes 13107200 | tf_op jit(solution)/shard_map/rbk,rkx->rbx/dot_general | solution.py:187
  690.4 11.3 reshape.517
  701.7 9.6 copy.158
  718.2 8.3 reshape_reshape.3
  726.4 30.8 %rev.34 = f32[2,2,128,3,1024]{2,1,4,3,0:T(2,128)} reverse(f32[2,2,128,3,1024]{2,1,4,3,0:T(2,128)} %reshape_reshape.3), dimensions={1} | reverse | bytes 12582912 | tf_op jit(solution)/shard_map/rev | solution.py:38
  757.3 10.6 copy.160
  767.9 77.8 %collective-permute-done.5 = f32[4,128,3,1024]{3,1,2,0:T(8,128)} collective-permute-done((f32[4,128,3,1024]{3,1,2,0:T(8,128)}, f32[4,128,3,1024]{3,1,2,0:T(8,128)}, u32[]{:S(2)}, u32[]{:S(2)}) %collective-permute-start.5) | collective-permute-done | bytes 6291488 | tf_op jit(solution)/shard_map/ppermute | solution.py:18
  852.2 13.8 %fusion.12 = f32[4,128,3,1024]{3,1,2,0:T(8,128)} fusion(f32[4,128,3,1024]{3,1,2,0:T(8,128)} %collective-permute-done.5, f32[2,2,128,3,1024]{4,2,3,1,0:T(8,128)} %rev.35, f32[2,2,128,3,1024]{4,2,3,1,0:T(8,128)} %copy.160, f32[4]{0:T(128)S(1)} %copy-done.26, pred[]{:T(512)S(6)} %eq.43, f32[4,128,3,1024]{3,2,1,0:T(4,128)} %reshape.517), kind=kLoop, calls=%fused_computation.20 | loop fusion | flops 11010048 | bytes 31457296 | tf_op jit(solution)/shard_map/jit(_where)/select_n | solution.py:65
  873.2 126.1 %collective-permute-done.6 = f32[4,128,3,1024]{3,1,2,0:T(8,128)} collective-permute-done((f32[4,128,3,1024]{3,1,2,0:T(8,128)}, f32[4,128,3,1024]{3,1,2,0:T(8,128)}, u32[]{:S(2)}, u32[]{:S(2)}) %collective-permute-start.6) | collective-permute-done | bytes 6291488 | tf_op jit(solution)/shard_map/ppermute | solution.py:18
  1005.9 13.0 fusion.7
  1030.4 124.7 %collective-permute-done.7 = f32[4,128,3,1024]{3,1,2,0:T(8,128)} collective-permute-done((f32[4,128,3,1024]{3,1,2,0:T(8,128)}, f32[4,128,3,1024]{3,1,2,0:T(8,128)}, u32[]{:S(2)}, u32[]{:S(2)}) %collective-permute-start.7) | collective-permute-done | bytes 6291488 | tf_op jit(solution)/shard_map/ppermute | solution.py:18
  1161.6 10.2 fusion.2
  1181.7 62.8 %collective-permute-done.8 = f32[128,3,1024]{2,0,1:T(8,128)} collective-permute-done((f32[128,3,1024]{2,0,1:T(8,128)}, f32[128,3,1024]{2,0,1:T(8,128)}, u32[]{:S(2)}, u32[]{:S(2)}) %collective-permute-start.8) | collective-permute-done | bytes 1572896 | tf_op jit(solution)/shard_map/ppermute | solution.py:18
  1257.2 74.0 %all-reduce = (f32[3,3,1024]{2,0,1:T(4,128)S(1)}, f32[1024]{0:T(1024)}) all-reduce(f32[3,3,1024]{2,0,1:T(4,128)S(1)} %pad_maximum_fusion.6, f32[1024]{0:T(1024)S(1)} %get-tuple-element.60), channel_id=1, replica_groups=mesh['seq'=16,'ch'=2] {'seq'}, use_global_device_ids=true, to_apply=%region_3.4 | all-reduce | flops 10240 | bytes 81920 | tf_op jit(solution)/shard_map/psum | solution.py:222
  (125 shorter events, 147.5 us)
Async XLA Ops:
  0.6 11.3 copy-start.14
  0.6 11.5 copy-start.13
  1.5 6.2 collective-permute-start
  7.3 5.9 copy-start.17
  7.3 5.8 copy-start.19
  7.3 11.8 copy-start.28
  12.1 7.6 copy-start.11
  12.1 43.3 %copy-start.9 = (bf16[128,1024]{1,0:T(8,128)(2,1)}, bf16[128,1024]{1,0:T(8,128)(2,1)S(1)}, u32[]{:S(2)}) copy-start(bf16[128,1024]{1,0:T(8,128)(2,1)S(1)} %get-tuple-element.51) | copy-start | bytes 786436
  13.2 38.8 %collective-permute-start.1 = (bf16[128,3,1024]{2,0,1:T(8,128)(2,1)}, bf16[128,3,1024]{2,0,1:T(8,128)(2,1)}, u32[]{:S(2)}, u32[]{:S(2)}) collective-permute-start(bf16[128,3,1024]{2,0,1:T(8,128)(2,1)} %pad_maximum_fusion.5), channel_id=1, source_target_pairs={{0,16},{2,18},{4,20},{6,22},{8,24},{10,26},{12,28},{14,30},{16,0},... | collective-permute-start | bytes 2359304 | tf_op jit(solution)/shard_map/ppermute | solution.py:18
  21.1 37.9 %copy-start.3 = (f32[1,128,3,1024]{3,1,2,0:T(8,128)}, f32[1,128,3,1024]{3,1,2,0:T(8,128)S(1)}, u32[]{:S(2)}) copy-start(f32[1,128,3,1024]{3,1,2,0:T(8,128)S(1)} %get-tuple-element.59) | copy-start | bytes 4718596
  73.0 136.7 %collective-permute-start.2 = (f32[4,128,3,1024]{3,1,2,0:T(8,128)}, f32[4,128,3,1024]{3,1,2,0:T(8,128)}, u32[]{:S(2)}, u32[]{:S(2)}) collective-permute-start(f32[4,128,3,1024]{3,1,2,0:T(8,128)} %fusion.22), channel_id=1, source_target_pairs={{0,8},{2,10},{4,12},{6,14},{8,0},{10,2},{12,4},{14,6},{16,24},{18,... | collective-permute-start | bytes 18874376 | tf_op jit(solution)/shard_map/ppermute | solution.py:18
  241.6 136.2 %collective-permute-start.3 = (f32[4,128,3,1024]{3,1,2,0:T(8,128)}, f32[4,128,3,1024]{3,1,2,0:T(8,128)}, u32[]{:S(2)}, u32[]{:S(2)}) collective-permute-start(f32[4,128,3,1024]{3,1,2,0:T(8,128)} %fusion.20), channel_id=1, source_target_pairs={{0,4},{2,6},{4,0},{6,2},{8,12},{10,14},{12,8},{14,10},{16,20},{18,... | collective-permute-start | bytes 18874376 | tf_op jit(solution)/shard_map/ppermute | solution.py:18
  408.5 135.2 %collective-permute-start.4 = (f32[4,128,3,1024]{3,1,2,0:T(8,128)}, f32[4,128,3,1024]{3,1,2,0:T(8,128)}, u32[]{:S(2)}, u32[]{:S(2)}) collective-permute-start(f32[4,128,3,1024]{3,1,2,0:T(8,128)} %fusion.18), channel_id=1, source_target_pairs={{0,2},{2,0},{4,6},{6,4},{8,10},{10,8},{12,14},{14,12},{16,18},{18,... | collective-permute-start | bytes 18874376 | tf_op jit(solution)/shard_map/ppermute | solution.py:18
  553.1 6.6 copy-start.27
  663.3 9.1 copy-start.16
  711.3 134.3 %collective-permute-start.5 = (f32[4,128,3,1024]{3,1,2,0:T(8,128)}, f32[4,128,3,1024]{3,1,2,0:T(8,128)}, u32[]{:S(2)}, u32[]{:S(2)}) collective-permute-start(f32[4,128,3,1024]{3,1,2,0:T(8,128)} %copy.158), channel_id=1, source_target_pairs={{0,2},{2,0},{4,6},{6,4},{8,10},{10,8},{12,14},{14,12},{16,18},{18,... | collective-permute-start | bytes 18874376 | tf_op jit(solution)/shard_map/ppermute | solution.py:18
  845.6 6.5 copy-start.26
  866.0 133.4 %collective-permute-start.6 = (f32[4,128,3,1024]{3,1,2,0:T(8,128)}, f32[4,128,3,1024]{3,1,2,0:T(8,128)}, u32[]{:S(2)}, u32[]{:S(2)}) collective-permute-start(f32[4,128,3,1024]{3,1,2,0:T(8,128)} %fusion.12), channel_id=1, source_target_pairs={{0,4},{2,6},{4,0},{6,2},{8,12},{10,14},{12,8},{14,10},{16,20},{18,... | collective-permute-start | bytes 18874376 | tf_op jit(solution)/shard_map/ppermute | solution.py:18
  999.3 6.6 copy-start.25
  1018.9 136.2 %collective-permute-start.7 = (f32[4,128,3,1024]{3,1,2,0:T(8,128)}, f32[4,128,3,1024]{3,1,2,0:T(8,128)}, u32[]{:S(2)}, u32[]{:S(2)}) collective-permute-start(f32[4,128,3,1024]{3,1,2,0:T(8,128)} %fusion.7), channel_id=1, source_target_pairs={{0,8},{2,10},{4,12},{6,14},{8,0},{10,2},{12,4},{14,6},{16,24},{18,... | collective-permute-start | bytes 18874376 | tf_op jit(solution)/shard_map/ppermute | solution.py:18
  1155.1 6.6 copy-start.24
  1176.5 72.3 %copy-start.8 = (f32[3,128,1024]{2,1,0:T(8,128)S(1)}, f32[3,128,1024]{2,1,0:T(8,128)}, u32[]{:S(2)}) copy-start(f32[3,128,1024]{2,1,0:T(8,128)} %copy-done.7) | copy-start | bytes 4718596
  1176.5 72.3 %copy-start.10 = (bf16[128,1024]{1,0:T(8,128)(2,1)S(1)}, bf16[128,1024]{1,0:T(8,128)(2,1)}, u32[]{:S(2)}) copy-start(bf16[128,1024]{1,0:T(8,128)(2,1)} %copy-done.9) | copy-start | bytes 786436
  1176.5 72.3 %copy-start.12 = (bf16[128,1024]{1,0:T(8,128)(2,1)S(1)}, bf16[128,1024]{1,0:T(8,128)(2,1)}, u32[]{:S(2)}) copy-start(bf16[128,1024]{1,0:T(8,128)(2,1)} %copy-done.11) | copy-start | bytes 786436
  1176.5 72.3 %copy-start.15 = (bf16[128,1024]{1,0:T(8,128)(2,1)S(1)}, bf16[128,1024]{1,0:T(8,128)(2,1)}, u32[]{:S(2)}) copy-start(bf16[128,1024]{1,0:T(8,128)(2,1)} %param.23) | copy-start | bytes 786436
  1176.5 72.3 %copy-start.23 = (f32[1024]{0:T(1024)S(1)}, f32[1024]{0:T(1024)}, u32[]{:S(2)}) copy-start(f32[1024]{0:T(1024)} %param.22) | copy-start | bytes 12292
  1176.5 68.0 %collective-permute-start.8 = (f32[128,3,1024]{2,0,1:T(8,128)}, f32[128,3,1024]{2,0,1:T(8,128)}, u32[]{:S(2)}, u32[]{:S(2)}) collective-permute-start(f32[128,3,1024]{2,0,1:T(8,128)} %fusion.29), channel_id=1, source_target_pairs={{0,16},{2,18},{4,20},{6,22},{8,24},{10,26},{12,28},{14,30},{16,0},... | collective-permute-start | bytes 4718600 | tf_op jit(solution)/shard_map/ppermute | solution.py:18
  1248.8 7.2 copy-start.1
  1248.9 7.2 copy-start.18
  1248.9 7.2 copy-start.20
  1248.9 7.2 copy-start.22
  1250.1 5.7 collective-permute-start.9
  (7 other events, 23.7 us)
where the time goes:
time: 1340 us; the launch traced here: 1330 us
  waiting for transfers between devices  831 us (62%)
  local copies, waits for them, and re-layouts  220 us (16%)
  other arithmetic  150 us (11%)
  blocking collectives  74 us (6%)
  matrix products  31.6 us (2%)
  starting transfers between devices  23.5 us (2%)
    ppermute x8, waiting for transfers between devices, swapped(): lax.ppermute(array, axis, [(i, i ^ 1 << apart) for i in range(lax.axis_si...  827 us
    rev x11, local copies, waits for them, and re-layouts, rotate_pair(): flipped = values.reshape((2, 2) + shape_rest)[:, ::-1].reshape(values.shape)  100 us
    psum x1, blocking collectives, per_device(): grad_taps, grad_skip = lax.psum((grad_taps_local, grad_skip_local), 'seq')  74 us
    select_n x4, other arithmetic, forward_section(): jnp.where(is_upper, rotate_pair(partner_vals - current, cosine, sine_part...  52.6 us
    select_n x3, other arithmetic, inverse_section(): jnp.where(is_upper, partner_vals - rotate_pair(current, cosine, -sine_par...  37 us
    sub x4, other arithmetic, forward_section(): partner_vals - current  32.3 us
  transfers between devices with their start and end apart: 10, of which 10 were waited for; matrix products, arithmetic and copies ran while one was open for 6% of the time, Pallas kernels for 0%

commit v1 on v0

v1 whole, which is shorter than its diff:
```python
import math

import jax
import jax.numpy as jnp
import ml_dtypes
import numpy as np
from jax import lax
from jax.experimental import pallas as pl
from jax.experimental.pallas import tpu as pltpu
from jax.sharding import PartitionSpec as P

HALF = 64
LANES = 2 * HALF
EXTRA = 16


def root(top, bottom):
    angle = math.pi * top / bottom
    return math.cos(angle), math.sin(angle)


def padded_dft(xs):
    m = len(xs)
    if m == 1:
        return [(xs[0], None), (xs[0], None)]
    even, odd = padded_dft(xs[0::2]), padded_dft(xs[1::2])
    out = [None] * (m + 1)
    for k in range(m // 2 + 1):
        (ar, ai), (br, bi) = even[k], odd[k]
        if k == 0:
            out[0], out[m] = (ar + br, None), (ar - br, None)
        elif 2 * k == m:
            out[k] = (ar, -br)
        else:
            c, s = root(k, m)
            if bi is None:
                tr, ti = br * c, br * -s
            else:
                tr, ti = br * c + bi * s, bi * c - br * s
            out[k] = (ar + tr, ti if ai is None else ai + ti)
            out[m - k] = (ar - tr, ti if ai is None else ti - ai)
    return out


def folded_sum(ys):
    m = len(ys) - 1
    if m == 1:
        return [ys[0][0] + ys[1][0]]
    even, odd = [], []
    for k in range(m // 2 + 1):
        (ar, ai), (br, bi) = ys[k], ys[m - k]
        if k == 0:
            even.append((ar + br, None))
            odd.append((ar - br, None))
        elif 2 * k == m:
            even.append((ar, None))
            odd.append((-ai, None))
        else:
            c, s = root(k, m)
            dr, di = ar - br, ai + bi
            even.append((ar + br, ai - bi))
            odd.append((dr * c - di * s, dr * s + di * c))
    out = [None] * m
    out[0::2], out[1::2] = folded_sum(even), folded_sum(odd)
    return out


def split_pair(values):
    high = values.astype(ml_dtypes.bfloat16)
    low = (values - high.astype(np.float64)).astype(ml_dtypes.bfloat16)
    return np.concatenate([high, low], axis=-1)


def dft_tables(blocks, tokens):
    period = 2 * blocks * tokens
    k1 = np.arange(blocks + 1)[:, None, None]
    k2 = np.arange(tokens)[None, :, None]
    place = np.arange(tokens)[None, None, :]
    angle = (2.0 * math.pi / period) * ((place * (k1 + 2 * blocks * k2)) % period)
    c, s = np.cos(angle), np.sin(angle)
    weight = np.where((k1 == 0) | (k1 == blocks), 1.0, 2.0) / period
    forward = np.concatenate([c, s], 2)
    inverse = np.concatenate([c.transpose(0, 2, 1), -s.transpose(0, 2, 1)], 2) * weight
    return split_pair(forward), split_pair(inverse)


def halves_swapped(values):
    return pltpu.roll(values, HALF, 1)


def interleave(first, second):
    low = lax.broadcasted_iota(jnp.int32, first.shape, 1) < HALF
    return (
        jnp.where(low, first, halves_swapped(second)),
        jnp.where(low, halves_swapped(first), second),
    )


def pack_kernel(one, two, value, filt, grad, out):
    tokens = one.shape[0]
    half = tokens // 2
    for pair in range(one.shape[1] // LANES):
        cols = slice(pair * LANES, (pair + 1) * LANES)
        tile = [ref[:, cols].astype(jnp.float32) for ref in (two, one, value, grad, filt)]
        parts = (
            (0, tokens, tile[0], tile[1]),
            (tokens, tokens, tile[2], tile[3]),
            (2 * tokens, half, tile[4][:half], tile[4][half:]),
        )
        for start, rows, first, second in parts:
            for side, piece in enumerate(interleave(first, second)):
                out[2 * pair + side, start : start + rows] = piece.astype(out.dtype)


def window_conv(window, weights, tokens):
    total = weights[0] * window[8 : 8 + tokens]
    for j in (1, 2):
        total = total + weights[j] * window[8 - j : 8 - j + tokens]
    return total


def owner_kernel(blocks, chunk, weights, ftab, itab, out, ug_ref, spec_ref, lg_ref, gf_ref, acc_ref):
    step = pl.program_id(0)
    tokens = ftab.shape[1]
    half = tokens // 2
    f32 = jnp.float32

    def block_rows(a, start):
        return chunk[a, start : start + tokens].astype(f32)

    def window(a, start):
        before = chunk[jnp.maximum(a - 1, 0), start + tokens - 16 : start + tokens].astype(f32)[8:]
        return jnp.concatenate([jnp.where(a > 0, before, 0.0), block_rows(a, start)], axis=0)

    w1 = [weights[j : j + 1] for j in range(3)]
    w2 = [weights[3 + j : 4 + j] for j in range(3)]

    @pl.when(step == 0)
    def _():
        @pl.loop(0, blocks)
        def _(a):
            c1 = window_conv(window(a, 0), w1, tokens)
            c2 = window_conv(window(a, tokens), w2, tokens)
            ug_ref[a] = (c1 * c2).astype(jnp.bfloat16).astype(f32)

        @pl.loop(0, tokens // 8)
        def _(r):
            at = pl.multiple_of(r * 8, 8)
            spectrum = padded_dft([ug_ref[a, pl.ds(at, 8)] for a in range(blocks)])
            for k, (real, imag) in enumerate(spectrum):
                spec_ref[k, pl.ds(at, 8), :LANES] = real
                spec_ref[k, pl.ds(tokens + at, 8), :LANES] = (
                    jnp.zeros_like(real) if imag is None else imag
                )

        @pl.loop(0, half // 16)
        def _(r):
            at = pl.multiple_of(r * 16, 16)
            tiles = [chunk[a, pl.ds(2 * tokens + at, 16)].astype(f32) for a in range(blocks)]
            low = lax.broadcasted_iota(jnp.int32, (8, LANES), 1) < HALF
            for sub in range(2):
                spectrum = padded_dft([t[8 * sub : 8 * sub + 8] for t in tiles])
                for k, pair in enumerate(spectrum):
                    for place, part in enumerate(pair):
                        part = jnp.zeros_like(pair[0]) if part is None else part
                        turned = halves_swapped(part)
                        row = place * tokens + at + 8 * sub
                        spec_ref[k, pl.ds(row, 8), LANES:] = jnp.where(low, part, turned)
                        spec_ref[k, pl.ds(row + half, 8), LANES:] = jnp.where(low, turned, part)

    def transform(table, values):
        high = values.astype(jnp.bfloat16)
        rest = (values - high.astype(f32)).astype(jnp.bfloat16)
        cos_high, sin_high, cos_low, sin_low = [
            table[0, :, i * tokens : (i + 1) * tokens] for i in range(4)
        ]
        left = jnp.concatenate(
            [
                jnp.concatenate([cos_high, sin_high, cos_low, sin_low], 1),
                jnp.concatenate([-sin_high, cos_high, -sin_low, cos_low], 1),
            ],
            0,
        )
        return jnp.dot(
            left, jnp.concatenate([high, high], 0), preferred_element_type=f32
        ) + jnp.dot(left[:, : 2 * tokens], rest, preferred_element_type=f32)

    spectral = transform(ftab, spec_ref[step])
    sign = jnp.where(lax.broadcasted_iota(jnp.int32, (tokens, LANES), 1) < HALF, 1.0, -1.0)
    ur, ui = spectral[:tokens, :LANES], spectral[tokens:, :LANES]
    hr, hi = spectral[:tokens, LANES:], spectral[tokens:, LANES:] * sign
    vr, vi = halves_swapped(ur), halves_swapped(ui)
    products = jnp.concatenate(
        [
            jnp.concatenate([ur * hr - ui * hi, ur * vr + ui * vi], 1),
            jnp.concatenate([ui * hr + ur * hi, vi * ur - vr * ui], 1),
        ],
        0,
    )
    spec_ref[step] = transform(itab, products)

    @pl.when(step == blocks)
    def _():
        skip = weights[6:7]
        low = lax.broadcasted_iota(jnp.int32, (8, LANES), 1) < HALF

        @pl.loop(0, tokens // 8)
        def _(r):
            at = pl.multiple_of(r * 8, 8)
            ys = [
                (spec_ref[k, pl.ds(at, 8), :LANES], spec_ref[k, pl.ds(tokens + at, 8), :LANES])
                for k in range(blocks + 1)
            ]
            for a, total in enumerate(folded_sum(ys)):
                lg_ref[a, pl.ds(at, 8)] = total + skip * ug_ref[a, pl.ds(at, 8)]

        @pl.loop(0, half // 8)
        def _(r):
            at = pl.multiple_of(r * 8, 8)
            ys = []
            for k in range(blocks + 1):
                pair = []
                for place in range(2):
                    row = place * tokens + at
                    top = spec_ref[k, pl.ds(row, 8), LANES:]
                    bottom = spec_ref[k, pl.ds(row + half, 8), LANES:]
                    pair.append(jnp.where(low, top, halves_swapped(bottom)))
                ys.append(tuple(pair))
            for a, total in enumerate(folded_sum(ys)):
                gf_ref[a, pl.ds(at, 8)] = total

        acc_ref[...] = jnp.zeros_like(acc_ref)

        def folded(values):
            total = values[:8]
            for r in range(1, tokens // 8):
                total = total + values[8 * r : 8 * r + 8]
            return total

        @pl.loop(0, blocks)
        def _(i):
            a = blocks - 1 - i
            one, two = window(a, 0), window(a, tokens)
            c1, c2 = window_conv(one, w1, tokens), window_conv(two, w2, tokens)
            lg = lg_ref[a]
            turned = halves_swapped(lg)
            x1, x2 = c2 * turned, c1 * turned
            ug = ug_ref[a]
            for j in range(3):
                acc_ref[j] += folded(x1 * one[8 - j : 8 - j + tokens])
                acc_ref[3 + j] += folded(x2 * two[8 - j : 8 - j + tokens])
            acc_ref[6] += folded(ug * halves_swapped(ug))
            after = acc_ref[7]
            out[a, :tokens] = lg.astype(out.dtype)
            out[a, tokens : tokens + half] = gf_ref[a].astype(out.dtype)
            out[a, tokens + half :] = jnp.concatenate(
                [after[:4], one[6:8], two[6:8], jnp.zeros((8, LANES), f32)], 0
            ).astype(out.dtype)
            acc_ref[7] = jnp.concatenate([x1[:2], x2[:2], jnp.zeros((4, LANES), f32)], 0)

        lower = lax.broadcasted_iota(jnp.int32, (1, LANES), 1) < HALF
        sums = [jnp.sum(acc_ref[j], axis=0, keepdims=True) for j in range(7)]
        sums[3] = jnp.where(lower, sums[3], sums[6])
        tail = jnp.concatenate(sums[:6] + [jnp.zeros((2, LANES), f32)], 0)

        @pl.loop(0, blocks)
        def _(a):
            rows = out[a, tokens + half :].astype(f32)
            out[a, tokens + half :] = jnp.concatenate([rows[:8], tail], 0).astype(out.dtype)


def finish(streams, cotangent, weights, low, high):
    tokens = streams[0].shape[0]
    half = tokens // 2
    at = tokens + half
    long_out, grad_mixed = low[:tokens], high[:tokens]
    grad_filter = jnp.concatenate([low[tokens:at], high[tokens:at]], 0)
    before = (high[at + 4 : at + 6], low[at + 4 : at + 6], low[at + 6 : at + 8])
    after = (high[at : at + 2], low[at : at + 2], low[at + 2 : at + 4])
    gates = []
    for s in range(3):
        window = jnp.concatenate([jnp.zeros_like(low[:6]), before[s], streams[s]], 0)
        gates.append(window_conv(window, [weights[3 * s + j] for j in range(3)], tokens))
    mixed_out = gates[0] * long_out
    conv_grads = (cotangent * long_out, grad_mixed * gates[2], grad_mixed * gates[1])
    grads = []
    for s in range(3):
        trailing = jnp.concatenate([conv_grads[s], after[s], jnp.zeros_like(low[:6])], 0)
        total = weights[3 * s] * trailing[:tokens]
        for j in (1, 2):
            total = total + weights[3 * s + j] * trailing[j : j + tokens]
        grads.append(total)
    sums = jnp.concatenate(
        [high[at + 8 : at + 11], low[at + 8 : at + 11], low[at + 11 : at + 14], high[at + 11 : at + 12]], 0
    )
    return [mixed_out] + grads + [grad_filter, sums]


def finish_kernel(one, two, value, grad, weights, back, *outs):
    rows = back.shape[1]
    for pair in range(one.shape[1] // LANES):
        cols = slice(pair * LANES, (pair + 1) * LANES)
        low, high = interleave(
            back[2 * pair].astype(jnp.float32), back[2 * pair + 1].astype(jnp.float32)
        )
        streams = [ref[:, cols].astype(jnp.float32) for ref in (one, two, value)]
        results = finish(
            streams,
            grad[:, cols].astype(jnp.float32),
            [weights[i : i + 1, cols] for i in range(9)],
            low,
            high,
        )
        for ref, result in zip(outs, results):
            ref[:, cols] = result.astype(ref.dtype)


VMEM = pl.BlockSpec(memory_space=pltpu.VMEM)


def per_device(stream_one, stream_two, stream_value, long_filter, short_taps, skip_gain, out_grad):
    blocks = lax.axis_size("seq")
    me = lax.axis_index("seq")
    tokens, channels = stream_one.shape
    half = tokens // 2
    owned = channels // blocks
    exact = owned == HALF
    bf16, f32 = jnp.bfloat16, jnp.float32
    rows_in = 2 * tokens + half
    rows_out = tokens + half + EXTRA
    taps_flat = short_taps.reshape(9, channels)

    def by_owner(array):
        split = array.reshape(array.shape[0], blocks, owned).transpose(1, 0, 2)
        return jnp.pad(split, ((0, 0), (0, 0), (0, HALF - owned)))

    def side_by_side(first, second):
        return jnp.concatenate([by_owner(first), by_owner(second)], 2)

    if exact:
        packed = pl.pallas_call(
            pack_kernel,
            out_shape=jax.ShapeDtypeStruct((blocks, rows_in, LANES), bf16),
            in_specs=[VMEM] * 5,
            out_specs=VMEM,
            name="pack",
        )(stream_one, stream_two, stream_value, long_filter, out_grad)
    else:
        packed = jnp.concatenate(
            [
                side_by_side(stream_two, stream_one),
                side_by_side(stream_value, out_grad),
                side_by_side(long_filter[:half], long_filter[half:]),
            ],
            1,
        )

    unit = jnp.zeros((3, channels), f32).at[0].set(1.0)
    lower = jnp.concatenate([taps_flat[3:9], skip_gain[None], skip_gain[None]], 0)
    upper = jnp.concatenate([taps_flat[:3], unit, skip_gain[None], skip_gain[None]], 0)
    weights = lax.dynamic_index_in_dim(side_by_side(lower, upper), me, 0, keepdims=False)

    owned_chunk = lax.all_to_all(packed, "seq", 0, 0, tiled=True)

    forward, inverse = dft_tables(blocks, tokens)
    size = 2 * tokens
    table_spec = pl.BlockSpec((1, tokens, 2 * size), lambda k: (k, 0, 0))

    def owner(*refs):
        owner_kernel(blocks, *refs)

    returned = pl.pallas_call(
        owner,
        out_shape=jax.ShapeDtypeStruct((blocks, rows_out, LANES), bf16),
        grid=(blocks + 1,),
        in_specs=[
            VMEM,
            VMEM,
            table_spec,
            table_spec,
        ],
        out_specs=VMEM,
        scratch_shapes=[
            pltpu.VMEM((blocks, tokens, LANES), f32),
            pltpu.VMEM((blocks + 1, size, 2 * LANES), f32),
            pltpu.VMEM((blocks, tokens, LANES), f32),
            pltpu.VMEM((blocks, half, LANES), f32),
            pltpu.VMEM((8, 8, LANES), f32),
        ],
        compiler_params=pltpu.CompilerParams(vmem_limit_bytes=58 * 1024 * 1024),
        name="owner",
    )(owned_chunk, weights, jnp.asarray(forward), jnp.asarray(inverse))

    back = lax.all_to_all(returned, "seq", 0, 0, tiled=True)

    if exact:
        shape = (tokens, channels)
        results = pl.pallas_call(
            finish_kernel,
            out_shape=[jax.ShapeDtypeStruct(shape, bf16)] * 4
            + [jax.ShapeDtypeStruct(shape, f32), jax.ShapeDtypeStruct((10, channels), f32)],
            in_specs=[VMEM] * 6,
            out_specs=[VMEM] * 6,
            name="finish",
        )(stream_one, stream_two, stream_value, out_grad, taps_flat, back)
    else:
        wide = back.astype(f32)

        def joined(part):
            return part[:, :, :owned].transpose(1, 0, 2).reshape(rows_out, channels)

        results = finish(
            [s.astype(f32) for s in (stream_one, stream_two, stream_value)],
            out_grad.astype(f32),
            [taps_flat[i : i + 1] for i in range(9)],
            joined(wide[:, :, :HALF]),
            joined(wide[:, :, HALF:]),
        )
        results = [r.astype(bf16) for r in results[:4]] + results[4:]
    mixed_out, grad_one, grad_two, grad_value, grad_filter, sums = results
    grad_taps = sums[:9].reshape(3, 3, channels)
    return (mixed_out, grad_one, grad_two, grad_value, grad_filter, grad_taps, sums[9])


def solution(mesh):
    rows = P("seq", "ch")
    return jax.shard_map(
        per_device,
        mesh=mesh,
        in_specs=(rows, rows, rows, rows, P(None, None, "ch"), P("ch"), rows),
        out_specs=(rows, rows, rows, rows, rows, P(None, None, "ch"), P("ch")),
        check_vma=False,
    )
```

time: 1340 us -> 100 us (0.07)
  waiting for transfers between devices: 831 us -> 47.6 us
  local copies, waits for them, and re-layouts: 220 us -> 5.78 us
  other arithmetic: 150 us -> 0.72 us
  blocking collectives: 74 us -> 0 us
  matrix products: 31.6 us -> 0 us
  Pallas kernels: 0 us -> 30 us
    ppermute x10 -> x0, waiting for transfers between devices: 831 us -> none  [the longest x8 827 us: swapped(): lax.ppermute(array, axis, [(i, i ^ 1 << apart) for i in range(lax.axis_si...]
    rev x11 -> x0, local copies, waits for them, and re-layouts: 100 us -> none  [rotate_pair(): flipped = values.reshape((2, 2) + shape_rest)[:, ::-1].reshape(values.shape)]
    select_n x8 -> x0, other arithmetic: 91.6 us -> none  [the longest x4 52.6 us: forward_section(): jnp.where(is_upper, rotate_pair(partner_vals - current, cosine, sine_part...]
    psum x1 -> x0, blocking collectives: 74 us -> none  [per_device(): grad_taps, grad_skip = lax.psum((grad_taps_local, grad_skip_local), 'seq')]
    reshape x6 -> x2, local copies, waits for them, and re-layouts: 60 us -> 2.12 us  [the longest x1 1.48 us: per_device(): grad_taps = sums[:9].reshape(3, 3, channels)]
    all_to_all x0 -> x2, waiting for transfers between devices: none -> 47.6 us  [the longest x1 28.4 us: per_device(): owned_chunk = lax.all_to_all(packed, 'seq', 0, 0, tiled=True)]
    sub x6 -> x0, other arithmetic: 36.7 us -> none  [the longest x4 32.3 us: forward_section(): partner_vals - current]
    dot_general x2 -> x0, matrix products: 31.6 us -> none  [the longest x1 18 us: per_device(): jnp.einsum('rbk,rkx->rbx', inverse_tab, products, precision=exact_mode, p...]
  transfers between devices with their start and end apart: 10 -> 2, of which waited for: 10 -> 2; matrix products, arithmetic and copies ran while one was open for 6% -> 2% of each run, Pallas kernels for 0% -> 0%
where the time goes in v1:
time: 100 us; the launch traced here: 99.7 us
  waiting for transfers between devices  47.6 us (48%)
  Pallas kernels  30 us (30%)
  starting transfers between devices  14.9 us (15%)
  local copies, waits for them, and re-layouts  5.78 us (6%)
    all_to_all x1, waiting for transfers between devices, per_device(): owned_chunk = lax.all_to_all(packed, 'seq', 0, 0, tiled=True)  28.4 us
    pallas_call x1, Pallas kernels, per_device(): pl.pallas_call(owner, out_shape=jax.ShapeDtypeStruct((blocks, rows_out, L...  23.1 us
    all_to_all x1, waiting for transfers between devices, per_device(): back = lax.all_to_all(returned, 'seq', 0, 0, tiled=True)  19.2 us
    all_to_all x1, starting transfers between devices, per_device(): owned_chunk = lax.all_to_all(packed, 'seq', 0, 0, tiled=True)  8.31 us
    all_to_all x1, starting transfers between devices, per_device(): back = lax.all_to_all(returned, 'seq', 0, 0, tiled=True)  6.57 us
    pallas_call x1, Pallas kernels, per_device(): pl.pallas_call(finish_kernel, out_shape=[jax.ShapeDtypeStruct(shape, bf16...  4.02 us
    pallas_call x1, Pallas kernels, per_device(): pl.pallas_call(pack_kernel, out_shape=jax.ShapeDtypeStruct((blocks, rows_...  2.89 us
    unnamed x10, local copies, waits for them, and re-layouts  2 us
  transfers between devices with their start and end apart: 2, of which 2 were waited for; matrix products, arithmetic and copies ran while one was open for 2% of the time, Pallas kernels for 0%

profile of v1, /device:TPU:0, one launch (start us, length us, event | category | flops | bytes accessed | tf_op | source)
XLA Modules:
  0.0 99.7 jit_solution(16892606508864291528)
XLA Ops:
  0.6 0.0 copy-start.3
  0.6 0.0 slice-start
  0.7 0.0 slice-start.1
  0.7 0.0 copy-start.4
  0.7 2.9 %pack.1 = bf16[16,320,128]{2,1,0:T(8,128)(2,1)} custom-call(bf16[128,1024]{1,0:T(8,128)(2,1)} %one.3, bf16[128,1024]{1,0:T(8,128)(2,1)} %two.3, bf16[128,1024]{1,0:T(8,128)(2,1)} %value.3, bf16[128,1024]{1,0:T(8,128)(2,1)} %filt.1, bf16[128,1024]{1,0:T(8,128)(2,1)} %grad.3), custom_call_target="tpu_custom_call" | custom-call | tf_op jit(solution)/shard_map/pack/pallas_call | solution.py:341
  3.6 8.3 %all-to-all-start = ((bf16[16,320,128]{2,1,0:T(8,128)(2,1)}), bf16[16,320,128]{2,1,0:T(8,128)(2,1)S(1)}, u32[]{:S(2)}, u32[]{:S(2)}) async-start(bf16[16,320,128]{2,1,0:T(8,128)(2,1)} %pack.1), calls=%async_computation | async-start | bytes 2621440 | tf_op jit(solution)/shard_map/all_to_all | solution.py:363
  11.9 0.0 slice-done
  11.9 0.1 concatenate.19
  12.0 0.0 slice-done.1
  12.0 0.1 concatenate.22
  12.1 0.0 copy-done.4
  12.1 0.1 concatenate.20
  12.2 0.0 copy-done.3
  12.3 0.7 fusion.3.refs_1_
  12.9 0.0 copy-start.2
  12.9 28.4 %all-to-all-done.refs_0_ = bf16[16,320,128]{2,1,0:T(8,128)(2,1)S(1)} async-done(((bf16[16,320,128]{2,1,0:T(8,128)(2,1)}), bf16[16,320,128]{2,1,0:T(8,128)(2,1)S(1)}, u32[]{:S(2)}, u32[]{:S(2)}) %all-to-all-start) | async-done | bytes 1310752 | tf_op jit(solution)/shard_map/all_to_all | solution.py:363
  41.4 0.0 copy-start
  41.4 1.1 %copy-done = bf16[16,320,128]{2,1,0:T(8,128)(2,1)} copy-done((bf16[16,320,128]{2,1,0:T(8,128)(2,1)}, bf16[16,320,128]{2,1,0:T(8,128)(2,1)S(1)}, u32[]{:S(2)}) %copy-start) | copy-done | bytes 1310744
  42.4 23.1 %owner.1 = bf16[16,208,128]{2,1,0:T(8,128)(2,1)} custom-call(bf16[16,320,128]{2,1,0:T(8,128)(2,1)} %copy-done, f32[8,128]{1,0:T(8,128)} %fusion.3.refs_1_, bf16[17,128,512]{2,1,0:T(8,128)(2,1)} %constant.49.clone.refs_2_, bf16[17,128,512]{2,1,0:T(8,128)(2,1)} %constant.50.clone.refs_3_), custom_call_target="tpu_custom_call" | custom-call | tf_op jit(solution)/shard_map/owner/pallas_call | solution.py:372
  65.5 6.6 %all-to-all-start.1 = ((bf16[16,208,128]{2,1,0:T(8,128)(2,1)}), bf16[16,208,128]{2,1,0:T(8,128)(2,1)S(1)}, u32[]{:S(2)}, u32[]{:S(2)}) async-start(bf16[16,208,128]{2,1,0:T(8,128)(2,1)} %owner.1), calls=%async_computation.1 | async-start | bytes 1703936 | tf_op jit(solution)/shard_map/all_to_all | solution.py:394
  72.1 0.0 copy-done.2
  72.1 0.6 reshape.59.weights
  72.7 19.2 %all-to-all-done.1.back = bf16[16,208,128]{2,1,0:T(8,128)(2,1)S(1)} async-done(((bf16[16,208,128]{2,1,0:T(8,128)(2,1)}), bf16[16,208,128]{2,1,0:T(8,128)(2,1)S(1)}, u32[]{:S(2)}, u32[]{:S(2)}) %all-to-all-start.1) | async-done | bytes 852000 | tf_op jit(solution)/shard_map/all_to_all | solution.py:394
  91.9 0.0 copy-start.1
  91.9 0.9 copy-done.1
  92.8 4.0 %finish.1 = (bf16[128,1024]{1,0:T(8,128)(2,1)}, bf16[128,1024]{1,0:T(8,128)(2,1)}, bf16[128,1024]{1,0:T(8,128)(2,1)}, bf16[128,1024]{1,0:T(8,128)(2,1)}, f32[128,1024]{1,0:T(8,128)}, /*index=5*/f32[10,1024]{1,0:T(8,128)}) custom-call(bf16[128,1024]{1,0:T(8,128)(2,1)} %one.3, bf16[128,1024]{1,0:T(8,128)(2,1)} %two.3, bf16[128,1024]{1,0:T(8,128)(2,1)} %value.3, ...), custom_call_target="tpu_custom_call" | custom-call | tf_op jit(solution)/shard_map/finish/pallas_call | solution.py:398
  96.8 1.4 %slice.31 = f32[1,1024]{1,0:T(1,128)} slice(f32[10,1024]{1,0:T(8,128)} %get-tuple-element.30), slice={[9:10], [0:1024]} | slice | bytes 8192 | tf_op jit(solution)/shard_map/slice | solution.py:422
  98.2 1.5 %reshape.60 = f32[3,3,1024]{2,1,0:T(4,128)} reshape(f32[9,1024]{1,0:T(8,128)} %bitcast.8) | data formatting | bytes 73728 | tf_op jit(solution)/shard_map/reshape | solution.py:421
  (3 shorter events, 0.1 us)
Async XLA Ops:
  0.6 11.6 %copy-start.3 = (f32[3,16,64]{2,0,1:T(4,128)S(1)}, f32[3,16,64]{2,0,1:T(4,128)}, u32[]{:S(2)}) copy-start(f32[3,16,64]{2,0,1:T(4,128)} %constant.44.clone.1) | copy-start | bytes 36868
  0.6 11.2 %slice-start = ((f32[3,3,1024]{2,1,0:T(4,128)}), f32[2,3,1024]{2,1,0:T(4,128)S(1)}, s32[]{:S(2)}) async-start(f32[3,3,1024]{2,1,0:T(4,128)} %param.15), calls=%async_computation.2 | async-start | bytes 65536 | tf_op jit(solution)/shard_map/slice | solution.py:359
  0.7 11.4 %slice-start.1 = ((f32[3,3,1024]{2,1,0:T(4,128)}), f32[1,3,1024]{2,1,0:T(4,128)S(1)}, s32[]{:S(2)}) async-start(f32[3,3,1024]{2,1,0:T(4,128)} %param.15), calls=%async_computation.3 | async-start | bytes 32768 | tf_op jit(solution)/shard_map/slice | solution.py:360
  0.7 11.5 %copy-start.4 = (f32[1024]{0:T(1024)S(1)}, f32[1024]{0:T(1024)}, u32[]{:S(2)}) copy-start(f32[1024]{0:T(1024)} %param.16) | copy-start | bytes 12292
  3.6 37.8 %all-to-all-start = ((bf16[16,320,128]{2,1,0:T(8,128)(2,1)}), bf16[16,320,128]{2,1,0:T(8,128)(2,1)S(1)}, u32[]{:S(2)}, u32[]{:S(2)}) async-start(bf16[16,320,128]{2,1,0:T(8,128)(2,1)} %pack.1), calls=%async_computation | async-start | bytes 2621440 | tf_op jit(solution)/shard_map/all_to_all | solution.py:363
  12.9 59.1 %copy-start.2 = (f32[3,3,1024]{2,1,0:T(4,128)S(1)}, f32[3,3,1024]{2,1,0:T(4,128)}, u32[]{:S(2)}) copy-start(f32[3,3,1024]{2,1,0:T(4,128)} %param.15) | copy-start | bytes 110596
  41.4 1.1 %copy-start = (bf16[16,320,128]{2,1,0:T(8,128)(2,1)}, bf16[16,320,128]{2,1,0:T(8,128)(2,1)S(1)}, u32[]{:S(2)}) copy-start(bf16[16,320,128]{2,1,0:T(8,128)(2,1)S(1)} %all-to-all-done.refs_0_) | copy-start | bytes 3932164
  65.5 26.4 %all-to-all-start.1 = ((bf16[16,208,128]{2,1,0:T(8,128)(2,1)}), bf16[16,208,128]{2,1,0:T(8,128)(2,1)S(1)}, u32[]{:S(2)}, u32[]{:S(2)}) async-start(bf16[16,208,128]{2,1,0:T(8,128)(2,1)} %owner.1), calls=%async_computation.1 | async-start | bytes 1703936 | tf_op jit(solution)/shard_map/all_to_all | solution.py:394
  91.9 0.9 copy-start.1

commit v2 on v1

--- a/solution.py
+++ b/solution.py
@@ -84,6 +84,14 @@
     return split_pair(forward), split_pair(inverse)
 
 
+def full_tables(tables):
+    parts = []
+    for pair in np.split(tables, 2, axis=-1):
+        cos, sin = np.split(pair, 2, axis=-1)
+        parts.append(np.concatenate([pair, np.concatenate([-sin, cos], -1)], -2))
+    return np.concatenate(parts, -1)
+
+
 def halves_swapped(values):
     return pltpu.roll(values, HALF, 1)
 
@@ -267,6 +275,192 @@
         def _(a):
             rows = out[a, tokens + half :].astype(f32)
             out[a, tokens + half :] = jnp.concatenate([rows[:8], tail], 0).astype(out.dtype)
+
+
+def resident_kernel(
+    blocks, chunk_hbm, weights, ftab_hbm, itab_hbm, out_hbm,
+    chunk, ftab, itab, high_ref, low_ref, zh_ref, zl_ref, spec_ref,
+    c1_ref, c2_ref, ug_ref, lg_ref, gf_ref, acc_ref, out, in_sems, tab_sems, out_sem,
+):
+    tokens = ftab.shape[1] // 2
+    size = 2 * tokens
+    half = tokens // 2
+    f32, bf16 = jnp.float32, jnp.bfloat16
+    pieces = in_sems.shape[0]
+    per = blocks // pieces
+
+    def piece_copy(p):
+        part = pl.ds(p * per, per)
+        return pltpu.make_async_copy(chunk_hbm.at[part], chunk.at[part], in_sems.at[p])
+
+    table_copies = [
+        pltpu.make_async_copy(ftab_hbm, ftab, tab_sems.at[0]),
+        pltpu.make_async_copy(itab_hbm, itab, tab_sems.at[1]),
+    ]
+    for p in range(pieces):
+        piece_copy(p).start()
+    for copy in table_copies:
+        copy.start()
+
+    def window(a, start):
+        before = chunk[jnp.maximum(a - 1, 0), start + tokens - 16 : start + tokens].astype(f32)[8:]
+        body = chunk[a, start : start + tokens].astype(f32)
+        return jnp.concatenate([jnp.where(a > 0, before, 0.0), body], axis=0)
+
+    w1 = [weights[j : j + 1] for j in range(3)]
+    w2 = [weights[3 + j : 4 + j] for j in range(3)]
+
+    for p in range(pieces):
+        piece_copy(p).wait()
+
+        @pl.loop(p * per, (p + 1) * per)
+        def _(a):
+            c1 = window_conv(window(a, 0), w1, tokens)
+            c2 = window_conv(window(a, tokens), w2, tokens)
+            c1_ref[a], c2_ref[a] = c1, c2
+            ug_ref[a] = (c1 * c2).astype(bf16)
+
+    def put(k, row, cols, values):
+        high = values.astype(bf16)
+        high_ref[k, pl.ds(row, 16), cols] = high
+        low_ref[k, pl.ds(row, 16), cols] = (values - high.astype(f32)).astype(bf16)
+
+    left, right = slice(0, LANES), slice(LANES, 2 * LANES)
+
+    @pl.loop(0, tokens // 16)
+    def _(r):
+        at = pl.multiple_of(r * 16, 16)
+        spectrum = padded_dft([ug_ref[a, pl.ds(at, 16)].astype(f32) for a in range(blocks)])
+        for k, (real, imag) in enumerate(spectrum):
+            put(k, at, left, real)
+            put(k, tokens + at, left, jnp.zeros_like(real) if imag is None else imag)
+
+    @pl.loop(0, half // 16)
+    def _(r):
+        at = pl.multiple_of(r * 16, 16)
+        low = lax.broadcasted_iota(jnp.int32, (16, LANES), 1) < HALF
+        spectrum = padded_dft(
+            [chunk[a, pl.ds(2 * tokens + at, 16)].astype(f32) for a in range(blocks)]
+        )
+        for k, pair in enumerate(spectrum):
+            for place, part in enumerate(pair):
+                part = jnp.zeros_like(pair[0]) if part is None else part
+                turned = halves_swapped(part)
+                put(k, place * tokens + at, right, jnp.where(low, part, turned))
+                put(k, place * tokens + half + at, right, jnp.where(low, turned, part))
+
+    for copy in table_copies:
+        copy.wait()
+
+    def apply(table, k, high, rest):
+        first = table[k, :, :size]
+        total = jnp.dot(first, high, preferred_element_type=f32)
+        total = total + jnp.dot(table[k, :, size:], high, preferred_element_type=f32)
+        return total + jnp.dot(first, rest, preferred_element_type=f32)
+
+    sign = jnp.where(lax.broadcasted_iota(jnp.int32, (1, LANES), 1) < HALF, 1.0, -1.0)
+
+    def into_products(k, slot):
+        spectral = apply(ftab, k, high_ref[k], low_ref[k])
+        ur, ui = spectral[:tokens, :LANES], spectral[tokens:, :LANES]
+        hr, hi = spectral[:tokens, LANES:], spectral[tokens:, LANES:] * sign
+        vr, vi = halves_swapped(ur), halves_swapped(ui)
+        for place, cols, values in (
+            (0, left, ur * hr - ui * hi),
+            (1, left, ui * hr + ur * hi),
+            (0, right, ur * vr + ui * vi),
+            (1, right, vi * ur - vr * ui),
+        ):
+            rows = slice(place * tokens, (place + 1) * tokens)
+            high = values.astype(bf16)
+            zh_ref[slot, rows, cols] = high
+            zl_ref[slot, rows, cols] = (values - high.astype(f32)).astype(bf16)
+
+    def out_of_products(k, slot):
+        spec_ref[k] = apply(itab, k, zh_ref[slot], zl_ref[slot])
+
+    into_products(0, 0)
+
+    @pl.loop(1, blocks + 1)
+    def _(k):
+        slot = lax.rem(k, 2)
+        out_of_products(k - 1, 1 - slot)
+        into_products(k, slot)
+
+    out_of_products(blocks, blocks % 2)
+
+    skip = weights[6:7]
+    low8 = lax.broadcasted_iota(jnp.int32, (8, LANES), 1) < HALF
+
+    @pl.loop(0, tokens // 16)
+    def _(r):
+        at = pl.multiple_of(r * 16, 16)
+        ug = [ug_ref[a, pl.ds(at, 16)].astype(f32) for a in range(blocks)]
+        for sub in range(2):
+            row = pl.multiple_of(at + 8 * sub, 8)
+            ys = [
+                (spec_ref[k, pl.ds(row, 8), left], spec_ref[k, pl.ds(tokens + row, 8), left])
+                for k in range(blocks + 1)
+            ]
+            for a, total in enumerate(folded_sum(ys)):
+                lg_ref[a, pl.ds(row, 8)] = total + skip * ug[a][8 * sub : 8 * sub + 8]
+
+    @pl.loop(0, half // 8)
+    def _(r):
+        at = pl.multiple_of(r * 8, 8)
+        ys = []
+        for k in range(blocks + 1):
+            pair = []
+            for place in range(2):
+                row = place * tokens + at
+                top = spec_ref[k, pl.ds(row, 8), right]
+                bottom = spec_ref[k, pl.ds(row + half, 8), right]
+                pair.append(jnp.where(low8, top, halves_swapped(bottom)))
+            ys.append(tuple(pair))
+        for a, total in enumerate(folded_sum(ys)):
+            gf_ref[a, pl.ds(at, 8)] = total
+
+    acc_ref[...] = jnp.zeros_like(acc_ref)
+
+    def folded(values):
+        total = values[:8]
+        for r in range(1, tokens // 8):
+            total = total + values[8 * r : 8 * r + 8]
+        return total
+
+    @pl.loop(0, blocks)
+    def _(i):
+        a = blocks - 1 - i
+        one, two = window(a, 0), window(a, tokens)
+        lg = lg_ref[a]
+        turned = halves_swapped(lg)
+        x1, x2 = c2_ref[a] * turned, c1_ref[a] * turned
+        ug = ug_ref[a].astype(f32)
+        for j in range(3):
+            acc_ref[j] += folded(x1 * one[8 - j : 8 - j + tokens])
+            acc_ref[3 + j] += folded(x2 * two[8 - j : 8 - j + tokens])
+        acc_ref[6] += folded(ug * halves_swapped(ug))
+        after = acc_ref[7]
+        out[a, :tokens] = lg.astype(out.dtype)
+        out[a, tokens : tokens + half] = gf_ref[a].astype(out.dtype)
+        out[a, tokens + half :] = jnp.concatenate(
+            [after[:4], one[6:8], two[6:8], jnp.zeros((8, LANES), f32)], 0
+        ).astype(out.dtype)
+        acc_ref[7] = jnp.concatenate([x1[:2], x2[:2], jnp.zeros((4, LANES), f32)], 0)
+
+    lower = lax.broadcasted_iota(jnp.int32, (1, LANES), 1) < HALF
+    sums = [jnp.sum(acc_ref[j], axis=0, keepdims=True) for j in range(7)]
+    sums[3] = jnp.where(lower, sums[3], sums[6])
+    tail = jnp.concatenate(sums[:6] + [jnp.zeros((2, LANES), f32)], 0)
+
+    @pl.loop(0, blocks)
+    def _(a):
+        rows = out[a, tokens + half :].astype(f32)
+        out[a, tokens + half :] = jnp.concatenate([rows[:8], tail], 0).astype(out.dtype)
+
+    copy = pltpu.make_async_copy(out, out_hbm, out_sem)
+    copy.start()
+    copy.wait()
 
 
 def finish(streams, cotangent, weights, low, high):
@@ -290,14 +484,11 @@
         for j in (1, 2):
             total = total + weights[3 * s + j] * trailing[j : j + tokens]
         grads.append(total)
-    sums = jnp.concatenate(
-        [high[at + 8 : at + 11], low[at + 8 : at + 11], low[at + 11 : at + 14], high[at + 11 : at + 12]], 0
-    )
-    return [mixed_out] + grads + [grad_filter, sums]
+    taps = [high[at + 8 : at + 11], low[at + 8 : at + 11], low[at + 11 : at + 14]]
+    return [mixed_out] + grads + [grad_filter] + taps + [high[at + 11 : at + 12]]
 
 
 def finish_kernel(one, two, value, grad, weights, back, *outs):
-    rows = back.shape[1]
     for pair in range(one.shape[1] // LANES):
         cols = slice(pair * LANES, (pair + 1) * LANES)
         low, high = interleave(
@@ -307,15 +498,19 @@
         results = finish(
             streams,
             grad[:, cols].astype(jnp.float32),
-            [weights[i : i + 1, cols] for i in range(9)],
+            [weights[i // 3, i % 3 : i % 3 + 1, cols] for i in range(9)],
             low,
             high,
         )
-        for ref, result in zip(outs, results):
+        for ref, result in zip(outs[:5], results[:5]):
             ref[:, cols] = result.astype(ref.dtype)
+        for s in range(3):
+            outs[5][s, :, cols] = results[5 + s]
+        outs[6][:, cols] = results[8]
 
 
 VMEM = pl.BlockSpec(memory_space=pltpu.VMEM)
+ANY = pl.BlockSpec(memory_space=pl.ANY)
 
 
 def per_device(stream_one, stream_two, stream_value, long_filter, short_taps, skip_gain, out_grad):
@@ -337,12 +532,16 @@
     def side_by_side(first, second):
         return jnp.concatenate([by_owner(first), by_owner(second)], 2)
 
+    steps = max(1, channels // 256)
+    by_columns = pl.BlockSpec((tokens, channels // steps), lambda i: (0, i))
+
     if exact:
         packed = pl.pallas_call(
             pack_kernel,
             out_shape=jax.ShapeDtypeStruct((blocks, rows_in, LANES), bf16),
-            in_specs=[VMEM] * 5,
-            out_specs=VMEM,
+            grid=(steps,),
+            in_specs=[by_columns] * 5,
+            out_specs=pl.BlockSpec((blocks // steps, rows_in, LANES), lambda i: (i, 0, 0)),
             name="pack",
         )(stream_one, stream_two, stream_value, long_filter, out_grad)
     else:
@@ -366,43 +565,86 @@
     size = 2 * tokens
     table_spec = pl.BlockSpec((1, tokens, 2 * size), lambda k: (k, 0, 0))
 
-    def owner(*refs):
-        owner_kernel(blocks, *refs)
-
-    returned = pl.pallas_call(
-        owner,
-        out_shape=jax.ShapeDtypeStruct((blocks, rows_out, LANES), bf16),
-        grid=(blocks + 1,),
-        in_specs=[
-            VMEM,
-            VMEM,
-            table_spec,
-            table_spec,
-        ],
-        out_specs=VMEM,
-        scratch_shapes=[
-            pltpu.VMEM((blocks, tokens, LANES), f32),
-            pltpu.VMEM((blocks + 1, size, 2 * LANES), f32),
-            pltpu.VMEM((blocks, tokens, LANES), f32),
-            pltpu.VMEM((blocks, half, LANES), f32),
-            pltpu.VMEM((8, 8, LANES), f32),
-        ],
-        compiler_params=pltpu.CompilerParams(vmem_limit_bytes=58 * 1024 * 1024),
-        name="owner",
-    )(owned_chunk, weights, jnp.asarray(forward), jnp.asarray(inverse))
+    if exact and blocks <= 16:
+        pieces = 4 if blocks % 4 == 0 else 1
+
+        def resident(*refs):
+            resident_kernel(blocks, *refs)
+
+        returned = pl.pallas_call(
+            resident,
+            out_shape=jax.ShapeDtypeStruct((blocks, rows_out, LANES), bf16),
+            in_specs=[ANY, VMEM, ANY, ANY],
+            out_specs=ANY,
+            scratch_shapes=[
+                pltpu.VMEM((blocks, rows_in, LANES), bf16),
+                pltpu.VMEM((blocks + 1, size, 2 * size), bf16),
+                pltpu.VMEM((blocks + 1, size, 2 * size), bf16),
+                pltpu.VMEM((blocks + 1, size, 2 * LANES), bf16),
+                pltpu.VMEM((blocks + 1, size, 2 * LANES), bf16),
+                pltpu.VMEM((2, size, 2 * LANES), bf16),
+                pltpu.VMEM((2, size, 2 * LANES), bf16),
+                pltpu.VMEM((blocks + 1, size, 2 * LANES), f32),
+                pltpu.VMEM((blocks, tokens, LANES), f32),
+                pltpu.VMEM((blocks, tokens, LANES), f32),
+                pltpu.VMEM((blocks, tokens, LANES), bf16),
+                pltpu.VMEM((blocks, tokens, LANES), f32),
+                pltpu.VMEM((blocks, half, LANES), f32),
+                pltpu.VMEM((8, 8, LANES), f32),
+                pltpu.VMEM((blocks, rows_out, LANES), bf16),
+                pltpu.SemaphoreType.DMA((pieces,)),
+                pltpu.SemaphoreType.DMA((2,)),
+                pltpu.SemaphoreType.DMA,
+            ],
+            compiler_params=pltpu.CompilerParams(vmem_limit_bytes=48 * 1024 * 1024),
+            name="owner",
+        )(
+            owned_chunk,
+            weights,
+            jnp.asarray(full_tables(forward)),
+            jnp.asarray(full_tables(inverse)),
+        )
+    else:
+
+        def owner(*refs):
+            owner_kernel(blocks, *refs)
+
+        returned = pl.pallas_call(
+            owner,
+            out_shape=jax.ShapeDtypeStruct((blocks, rows_out, LANES), bf16),
+            grid=(blocks + 1,),
+            in_specs=[VMEM, VMEM, table_spec, table_spec],
+            out_specs=VMEM,
+            scratch_shapes=[
+                pltpu.VMEM((blocks, tokens, LANES), f32),
+                pltpu.VMEM((blocks + 1, size, 2 * LANES), f32),
+                pltpu.VMEM((blocks, tokens, LANES), f32),
+                pltpu.VMEM((blocks, half, LANES), f32),
+                pltpu.VMEM((8, 8, LANES), f32),
+            ],
+            compiler_params=pltpu.CompilerParams(vmem_limit_bytes=58 * 1024 * 1024),
+            name="owner",
+        )(owned_chunk, weights, jnp.asarray(forward), jnp.asarray(inverse))
 
     back = lax.all_to_all(returned, "seq", 0, 0, tiled=True)
 
     if exact:
         shape = (tokens, channels)
+        taps_spec = pl.BlockSpec((3, 3, channels // steps), lambda i: (0, 0, i))
         results = pl.pallas_call(
             finish_kernel,
             out_shape=[jax.ShapeDtypeStruct(shape, bf16)] * 4
-            + [jax.ShapeDtypeStruct(shape, f32), jax.ShapeDtypeStruct((10, channels), f32)],
-            in_specs=[VMEM] * 6,
-            out_specs=[VMEM] * 6,
+            + [
+                jax.ShapeDtypeStruct(shape, f32),
+                jax.ShapeDtypeStruct(short_taps.shape, f32),
+                jax.ShapeDtypeStruct((1, channels), f32),
+            ],
+            grid=(steps,),
+            in_specs=[by_columns] * 4
+            + [taps_spec, pl.BlockSpec((blocks // steps, rows_out, LANES), lambda i: (i, 0, 0))],
+            out_specs=[by_columns] * 5 + [taps_spec, pl.BlockSpec((1, channels // steps), lambda i: (0, i))],
             name="finish",
-        )(stream_one, stream_two, stream_value, out_grad, taps_flat, back)
+        )(stream_one, stream_two, stream_value, out_grad, short_taps, back)
     else:
         wide = back.astype(f32)
 
@@ -416,10 +658,12 @@
             joined(wide[:, :, :HALF]),
             joined(wide[:, :, HALF:]),
         )
-        results = [r.astype(bf16) for r in results[:4]] + results[4:]
-    mixed_out, grad_one, grad_two, grad_value, grad_filter, sums = results
-    grad_taps = sums[:9].reshape(3, 3, channels)
-    return (mixed_out, grad_one, grad_two, grad_value, grad_filter, grad_taps, sums[9])
+        results = [r.astype(bf16) for r in results[:4]] + [
+            results[4],
+            jnp.stack(results[5:8]),
+            results[8],
+        ]
+    return tuple(results[:6]) + (results[6].reshape(channels),)
 
 
 def solution(mesh):

time: 100 us -> 90.5 us (0.905)
  blocking collectives: 0 us -> 28 us
  waiting for transfers between devices: 47.6 us -> 29 us
  starting transfers between devices: 14.9 us -> 8.31 us
  Pallas kernels: 30 us -> 23.5 us
  local copies, waits for them, and re-layouts: 5.78 us -> 0.31 us
    all_to_all x0 -> x1, blocking collectives: none -> 28 us  [per_device(): back = lax.all_to_all(returned, 'seq', 0, 0, tiled=True)]
    all_to_all x1 -> x0, waiting for transfers between devices: 19.2 us -> none  [per_device(): back = lax.all_to_all(returned, 'seq', 0, 0, tiled=True)]
    pallas_call x1, Pallas kernels: 23.1 us -> 15.4 us  [per_device(): pl.pallas_call(resident, out_shape=jax.ShapeDtypeStruct((blocks, rows_out...]
    all_to_all x1 -> x0, starting transfers between devices: 6.57 us -> none  [per_device(): back = lax.all_to_all(returned, 'seq', 0, 0, tiled=True)]
    reshape x2 -> x0, local copies, waits for them, and re-layouts: 2.12 us -> none  [the longest x1 1.48 us: per_device(): grad_taps = sums[:9].reshape(3, 3, channels)]
    unnamed x10 -> x4, local copies, waits for them, and re-layouts: 2 us -> 0.01 us
    slice x1 -> x0, local copies, waits for them, and re-layouts: 1.35 us -> none  [per_device(): sums[9]]
  transfers between devices with their start and end apart: 2 -> 1, of which waited for: 2 -> 1; matrix products, arithmetic and copies ran while one was open for 2% -> 0% of each run, Pallas kernels for 0% -> 0%
where the time goes in v2:
time: 90.5 us; the launch traced here: 90 us
  waiting for transfers between devices  29 us (32%)
  blocking collectives  28 us (31%)
  Pallas kernels  23.5 us (26%)
  starting transfers between devices  8.31 us (9%)
    all_to_all x1, waiting for transfers between devices, per_device(): owned_chunk = lax.all_to_all(packed, 'seq', 0, 0, tiled=True)  29 us
    all_to_all x1, blocking collectives, per_device(): back = lax.all_to_all(returned, 'seq', 0, 0, tiled=True)  28 us
    pallas_call x1, Pallas kernels, per_device(): pl.pallas_call(resident, out_shape=jax.ShapeDtypeStruct((blocks, rows_out...  15.4 us
    all_to_all x1, starting transfers between devices, per_device(): owned_chunk = lax.all_to_all(packed, 'seq', 0, 0, tiled=True)  8.31 us
    pallas_call x1, Pallas kernels, per_device(): pl.pallas_call(finish_kernel, out_shape=[jax.ShapeDtypeStruct(shape, bf16...  4.33 us
    pallas_call x1, Pallas kernels, per_device(): pl.pallas_call(pack_kernel, out_shape=jax.ShapeDtypeStruct((blocks, rows_...  3.74 us
  transfers between devices with their start and end apart: 1, of which 1 were waited for; matrix products, arithmetic and copies ran while one was open for 0% of the time, Pallas kernels for 0%

profile of v2, /device:TPU:0, one launch (start us, length us, event | category | flops | bytes accessed | tf_op | source)
XLA Modules:
  0.0 90.0 jit_solution(14462896355544406915)
XLA Ops:
  0.6 0.0 copy-start
  0.6 0.0 slice-start
  0.7 0.0 slice-start.1
  0.7 0.0 copy-start.1
  0.7 3.7 %pack.1 = bf16[16,320,128]{2,1,0:T(8,128)(2,1)} custom-call(bf16[128,1024]{1,0:T(8,128)(2,1)} %one.3, bf16[128,1024]{1,0:T(8,128)(2,1)} %two.3, bf16[128,1024]{1,0:T(8,128)(2,1)} %value.3, bf16[128,1024]{1,0:T(8,128)(2,1)} %filt.1, bf16[128,1024]{1,0:T(8,128)(2,1)} %grad.3), custom_call_target="tpu_custom_call" | custom-call | tf_op jit(solution)/shard_map/pack/pallas_call | solution.py:539
  4.4 8.3 %all-to-all-start = ((bf16[16,320,128]{2,1,0:T(8,128)(2,1)}), bf16[16,320,128]{2,1,0:T(8,128)(2,1)S(1)}, u32[]{:S(2)}, u32[]{:S(2)}) async-start(bf16[16,320,128]{2,1,0:T(8,128)(2,1)} %pack.1), calls=%async_computation | async-start | bytes 2621440 | tf_op jit(solution)/shard_map/all_to_all | solution.py:562
  12.7 0.0 copy-done.1
  12.8 0.1 concatenate.20
  12.8 0.0 slice-done
  12.8 0.1 concatenate.19
  13.0 0.0 slice-done.1
  13.0 0.1 concatenate.22
  13.1 0.0 copy-done
  13.1 0.1 fusion.3.refs_1_
  13.2 29.0 %all-to-all-done.refs_0_ = bf16[16,320,128]{2,1,0:T(8,128)(2,1)S(1)} async-done(((bf16[16,320,128]{2,1,0:T(8,128)(2,1)}), bf16[16,320,128]{2,1,0:T(8,128)(2,1)S(1)}, u32[]{:S(2)}, u32[]{:S(2)}) %all-to-all-start) | async-done | bytes 1310752 | tf_op jit(solution)/shard_map/all_to_all | solution.py:562
  42.2 15.4 %owner.1 = bf16[16,208,128]{2,1,0:T(8,128)(2,1)S(1)} custom-call(bf16[16,320,128]{2,1,0:T(8,128)(2,1)S(1)} %all-to-all-done.refs_0_, f32[8,128]{1,0:T(8,128)S(1)} %fusion.3.refs_1_, bf16[17,256,512]{2,1,0:T(8,128)(2,1)} %constant.49.clone.refs_2_, bf16[17,256,512]{2,1,0:T(8,128)(2,1)} %constant.50.clone.refs_3_), custom_call_target="tpu_custom_call" | custom-call | tf_op jit(solution)/shard_map/owner/pallas_call | solution.py:574
  57.7 28.0 %all_to_all.10.back = bf16[16,208,128]{2,1,0:T(8,128)(2,1)} all-to-all(bf16[16,208,128]{2,1,0:T(8,128)(2,1)S(1)} %owner.1), channel_id=1, replica_groups=mesh['seq'=16,'ch'=2] {'seq'}, dimensions={0} | all-to-all | bytes 1703936 | tf_op jit(solution)/shard_map/all_to_all | solution.py:629
  85.7 4.3 %finish.1 = (bf16[128,1024]{1,0:T(8,128)(2,1)}, bf16[128,1024]{1,0:T(8,128)(2,1)}, bf16[128,1024]{1,0:T(8,128)(2,1)}, bf16[128,1024]{1,0:T(8,128)(2,1)}, f32[128...) custom-call(bf16[128,1024]{1,0:T(8,128)(2,1)} %one.3, bf16[128,1024]{1,0:T(8,128)(2,1)} %two.3, ...), custom_call_target="tpu_custom_call" | custom-call | tf_op jit(solution)/shard_map/finish/pallas_call | solution.py:634
  (3 shorter events, 0.1 us)
Async XLA Ops:
  0.6 12.4 %copy-start = (f32[3,16,64]{2,0,1:T(4,128)S(1)}, f32[3,16,64]{2,0,1:T(4,128)}, u32[]{:S(2)}) copy-start(f32[3,16,64]{2,0,1:T(4,128)} %constant.44.clone.1) | copy-start | bytes 36868
  0.6 12.2 %slice-start = ((f32[3,3,1024]{2,1,0:T(4,128)}), f32[2,3,1024]{2,1,0:T(4,128)S(1)}, s32[]{:S(2)}) async-start(f32[3,3,1024]{2,1,0:T(4,128)} %weights.1), calls=%async_computation.2 | async-start | bytes 65536 | tf_op jit(solution)/shard_map/slice | solution.py:558
  0.7 12.3 %slice-start.1 = ((f32[3,3,1024]{2,1,0:T(4,128)}), f32[1,3,1024]{2,1,0:T(4,128)S(1)}, s32[]{:S(2)}) async-start(f32[3,3,1024]{2,1,0:T(4,128)} %weights.1), calls=%async_computation.3 | async-start | bytes 32768 | tf_op jit(solution)/shard_map/slice | solution.py:559
  0.7 12.1 %copy-start.1 = (f32[1024]{0:T(1024)S(1)}, f32[1024]{0:T(1024)}, u32[]{:S(2)}) copy-start(f32[1024]{0:T(1024)} %param.16) | copy-start | bytes 12292
  4.4 37.8 %all-to-all-start = ((bf16[16,320,128]{2,1,0:T(8,128)(2,1)}), bf16[16,320,128]{2,1,0:T(8,128)(2,1)S(1)}, u32[]{:S(2)}, u32[]{:S(2)}) async-start(bf16[16,320,128]{2,1,0:T(8,128)(2,1)} %pack.1), calls=%async_computation | async-start | bytes 2621440 | tf_op jit(solution)/shard_map/all_to_all | solution.py:562

commit v3 on v2

--- a/solution.py
+++ b/solution.py
@@ -84,14 +84,6 @@
     return split_pair(forward), split_pair(inverse)
 
 
-def full_tables(tables):
-    parts = []
-    for pair in np.split(tables, 2, axis=-1):
-        cos, sin = np.split(pair, 2, axis=-1)
-        parts.append(np.concatenate([pair, np.concatenate([-sin, cos], -1)], -2))
-    return np.concatenate(parts, -1)
-
-
 def halves_swapped(values):
     return pltpu.roll(values, HALF, 1)
 
@@ -278,28 +270,18 @@
 
 
 def resident_kernel(
-    blocks, chunk_hbm, weights, ftab_hbm, itab_hbm, out_hbm,
-    chunk, ftab, itab, high_ref, low_ref, zh_ref, zl_ref, spec_ref,
-    c1_ref, c2_ref, ug_ref, lg_ref, gf_ref, acc_ref, out, in_sems, tab_sems, out_sem,
+    blocks, chunk, weights, tables_hbm, out,
+    tables, high_ref, low_ref, zh_ref, zl_ref, spec_ref,
+    c1_ref, c2_ref, ug_ref, lg_ref, gf_ref, acc_ref, sems,
 ):
-    tokens = ftab.shape[1] // 2
+    tokens = tables.shape[2]
     size = 2 * tokens
     half = tokens // 2
     f32, bf16 = jnp.float32, jnp.bfloat16
-    pieces = in_sems.shape[0]
-    per = blocks // pieces
-
-    def piece_copy(p):
-        part = pl.ds(p * per, per)
-        return pltpu.make_async_copy(chunk_hbm.at[part], chunk.at[part], in_sems.at[p])
-
-    table_copies = [
-        pltpu.make_async_copy(ftab_hbm, ftab, tab_sems.at[0]),
-        pltpu.make_async_copy(itab_hbm, itab, tab_sems.at[1]),
+    copies = [
+        pltpu.make_async_copy(tables_hbm.at[i], tables.at[i], sems.at[i]) for i in range(2)
     ]
-    for p in range(pieces):
-        piece_copy(p).start()
-    for copy in table_copies:
+    for copy in copies:
         copy.start()
 
     def window(a, start):
@@ -310,15 +292,12 @@
     w1 = [weights[j : j + 1] for j in range(3)]
     w2 = [weights[3 + j : 4 + j] for j in range(3)]
 
-    for p in range(pieces):
-        piece_copy(p).wait()
-
-        @pl.loop(p * per, (p + 1) * per)
-        def _(a):
-            c1 = window_conv(window(a, 0), w1, tokens)
-            c2 = window_conv(window(a, tokens), w2, tokens)
-            c1_ref[a], c2_ref[a] = c1, c2
-            ug_ref[a] = (c1 * c2).astype(bf16)
+    @pl.loop(0, blocks)
+    def _(a):
+        c1 = window_conv(window(a, 0), w1, tokens)
+        c2 = window_conv(window(a, tokens), w2, tokens)
+        c1_ref[a], c2_ref[a] = c1, c2
+        ug_ref[a] = (c1 * c2).astype(bf16)
 
     def put(k, row, cols, values):
         high = values.astype(bf16)
@@ -349,19 +328,22 @@
                 put(k, place * tokens + at, right, jnp.where(low, part, turned))
                 put(k, place * tokens + half + at, right, jnp.where(low, turned, part))
 
-    for copy in table_copies:
-        copy.wait()
+    def whole_map(table, k, start):
+        pair = tables[table, k, :, start : start + size]
+        return jnp.concatenate(
+            [pair, jnp.concatenate([-pair[:, tokens:], pair[:, :tokens]], 1)], 0
+        )
 
     def apply(table, k, high, rest):
-        first = table[k, :, :size]
+        first = whole_map(table, k, 0)
         total = jnp.dot(first, high, preferred_element_type=f32)
-        total = total + jnp.dot(table[k, :, size:], high, preferred_element_type=f32)
+        total = total + jnp.dot(whole_map(table, k, size), high, preferred_element_type=f32)
         return total + jnp.dot(first, rest, preferred_element_type=f32)
 
     sign = jnp.where(lax.broadcasted_iota(jnp.int32, (1, LANES), 1) < HALF, 1.0, -1.0)
 
     def into_products(k, slot):
-        spectral = apply(ftab, k, high_ref[k], low_ref[k])
+        spectral = apply(0, k, high_ref[k], low_ref[k])
         ur, ui = spectral[:tokens, :LANES], spectral[tokens:, :LANES]
         hr, hi = spectral[:tokens, LANES:], spectral[tokens:, LANES:] * sign
         vr, vi = halves_swapped(ur), halves_swapped(ui)
@@ -377,17 +359,32 @@
             zl_ref[slot, rows, cols] = (values - high.astype(f32)).astype(bf16)
 
     def out_of_products(k, slot):
-        spec_ref[k] = apply(itab, k, zh_ref[slot], zl_ref[slot])
-
-    into_products(0, 0)
-
-    @pl.loop(1, blocks + 1)
-    def _(k):
-        slot = lax.rem(k, 2)
-        out_of_products(k - 1, 1 - slot)
-        into_products(k, slot)
-
-    out_of_products(blocks, blocks % 2)
+        spec_ref[k] = apply(1, k, zh_ref[slot], zl_ref[slot])
+
+    for copy in copies:
+        copy.wait()
+
+    group = zh_ref.shape[0] // 2
+    whole = (blocks + 1) // group
+    rest = range(whole * group, blocks + 1)
+    for j in range(group):
+        into_products(j, j)
+
+    @pl.loop(1, whole)
+    def _(i):
+        now = lax.rem(i, 2) * group
+        for j in range(group):
+            out_of_products((i - 1) * group + j, group - now + j)
+        for j in range(group):
+            into_products(i * group + j, now + j)
+
+    last = (whole - 1) % 2 * group
+    for j, k in enumerate(rest):
+        into_products(k, group - last + j)
+    for j in range(group):
+        out_of_products((whole - 1) * group + j, last + j)
+    for j, k in enumerate(rest):
+        out_of_products(k, group - last + j)
 
     skip = weights[6:7]
     low8 = lax.broadcasted_iota(jnp.int32, (8, LANES), 1) < HALF
@@ -435,11 +432,9 @@
         lg = lg_ref[a]
         turned = halves_swapped(lg)
         x1, x2 = c2_ref[a] * turned, c1_ref[a] * turned
-        ug = ug_ref[a].astype(f32)
         for j in range(3):
             acc_ref[j] += folded(x1 * one[8 - j : 8 - j + tokens])
             acc_ref[3 + j] += folded(x2 * two[8 - j : 8 - j + tokens])
-        acc_ref[6] += folded(ug * halves_swapped(ug))
         after = acc_ref[7]
         out[a, :tokens] = lg.astype(out.dtype)
         out[a, tokens : tokens + half] = gf_ref[a].astype(out.dtype)
@@ -449,34 +444,43 @@
         acc_ref[7] = jnp.concatenate([x1[:2], x2[:2], jnp.zeros((4, LANES), f32)], 0)
 
     lower = lax.broadcasted_iota(jnp.int32, (1, LANES), 1) < HALF
-    sums = [jnp.sum(acc_ref[j], axis=0, keepdims=True) for j in range(7)]
-    sums[3] = jnp.where(lower, sums[3], sums[6])
-    tail = jnp.concatenate(sums[:6] + [jnp.zeros((2, LANES), f32)], 0)
+    sums = [jnp.sum(acc_ref[j], axis=0, keepdims=True) for j in range(6)]
+    sums[3] = jnp.where(lower, sums[3], halves_swapped(gf_ref[0, :8])[:1])
+    tail = jnp.concatenate(sums + [jnp.zeros((2, LANES), f32)], 0)
 
     @pl.loop(0, blocks)
     def _(a):
         rows = out[a, tokens + half :].astype(f32)
         out[a, tokens + half :] = jnp.concatenate([rows[:8], tail], 0).astype(out.dtype)
 
-    copy = pltpu.make_async_copy(out, out_hbm, out_sem)
-    copy.start()
-    copy.wait()
-
-
-def finish(streams, cotangent, weights, low, high):
+
+def local_gates(streams, weights):
     tokens = streams[0].shape[0]
+    gates = []
+    for s, stream in enumerate(streams):
+        window = jnp.concatenate([jnp.zeros_like(stream[:8]), stream], 0)
+        gates.append(window_conv(window, weights[3 * s : 3 * s + 3], tokens))
+    return gates
+
+
+def finish(gates, cotangent, weights, low, high):
+    tokens = cotangent.shape[0]
     half = tokens // 2
     at = tokens + half
     long_out, grad_mixed = low[:tokens], high[:tokens]
     grad_filter = jnp.concatenate([low[tokens:at], high[tokens:at]], 0)
     before = (high[at + 4 : at + 6], low[at + 4 : at + 6], low[at + 6 : at + 8])
     after = (high[at : at + 2], low[at : at + 2], low[at + 2 : at + 4])
-    gates = []
+    whole = []
     for s in range(3):
-        window = jnp.concatenate([jnp.zeros_like(low[:6]), before[s], streams[s]], 0)
-        gates.append(window_conv(window, [weights[3 * s + j] for j in range(3)], tokens))
-    mixed_out = gates[0] * long_out
-    conv_grads = (cotangent * long_out, grad_mixed * gates[2], grad_mixed * gates[1])
+        older, newer = before[s][:1], before[s][1:]
+        w1, w2 = weights[3 * s + 1], weights[3 * s + 2]
+        missing = jnp.concatenate(
+            [w1 * newer + w2 * older, w2 * newer, jnp.zeros((6, older.shape[1]), jnp.float32)], 0
+        )
+        whole.append(jnp.concatenate([gates[s][:8] + missing, gates[s][8:]], 0))
+    mixed_out = whole[0] * long_out
+    conv_grads = (cotangent * long_out, grad_mixed * whole[2], grad_mixed * whole[1])
     grads = []
     for s in range(3):
         trailing = jnp.concatenate([conv_grads[s], after[s], jnp.zeros_like(low[:6])], 0)
@@ -488,29 +492,57 @@
     return [mixed_out] + grads + [grad_filter] + taps + [high[at + 11 : at + 12]]
 
 
-def finish_kernel(one, two, value, grad, weights, back, *outs):
+def gates_kernel(one, two, value, weights, after, gates):
+    del after
     for pair in range(one.shape[1] // LANES):
         cols = slice(pair * LANES, (pair + 1) * LANES)
-        low, high = interleave(
-            back[2 * pair].astype(jnp.float32), back[2 * pair + 1].astype(jnp.float32)
+        results = local_gates(
+            [ref[:, cols].astype(jnp.float32) for ref in (one, two, value)],
+            [weights[i // 3, i % 3 : i % 3 + 1, cols] for i in range(9)],
         )
-        streams = [ref[:, cols].astype(jnp.float32) for ref in (one, two, value)]
-        results = finish(
-            streams,
-            grad[:, cols].astype(jnp.float32),
-            [weights[i // 3, i % 3 : i % 3 + 1, cols] for i in range(9)],
-            low,
-            high,
-        )
-        for ref, result in zip(outs[:5], results[:5]):
-            ref[:, cols] = result.astype(ref.dtype)
-        for s in range(3):
-            outs[5][s, :, cols] = results[5 + s]
-        outs[6][:, cols] = results[8]
+        for s, result in enumerate(results):
+            gates[s, :, cols] = result
+
+
+def finish_kernel(gates, grad, weights, back, *refs):
+    targets, grad_taps, grad_skip = refs[:5], refs[5], refs[6]
+    buffers, sems = refs[7:12], refs[12]
+    pieces = sems.shape[1]
+    width = grad.shape[1] // pieces
+
+    def copy(i, piece):
+        cols = pl.ds(piece * width, width)
+        return pltpu.make_async_copy(buffers[i].at[:, cols], targets[i].at[:, cols], sems.at[i, piece])
+
+    for piece in range(pieces):
+        for start in range(piece * width, (piece + 1) * width, LANES):
+            cols = slice(start, start + LANES)
+            owner = start // HALF
+            low, high = interleave(
+                back[owner].astype(jnp.float32), back[owner + 1].astype(jnp.float32)
+            )
+            results = finish(
+                [gates[s, :, cols] for s in range(3)],
+                grad[:, cols].astype(jnp.float32),
+                [weights[i // 3, i % 3 : i % 3 + 1, cols] for i in range(9)],
+                low,
+                high,
+            )
+            for ref, result in zip(buffers, results[:5]):
+                ref[:, cols] = result.astype(ref.dtype)
+            for s in range(3):
+                grad_taps[s, :, cols] = results[5 + s]
+            grad_skip[:, cols] = results[8]
+        for i in range(5):
+            copy(i, piece).start()
+    for piece in range(pieces):
+        for i in range(5):
+            copy(i, piece).wait()
 
 
 VMEM = pl.BlockSpec(memory_space=pltpu.VMEM)
 ANY = pl.BlockSpec(memory_space=pl.ANY)
+HBM = pl.BlockSpec(memory_space=pltpu.HBM)
 
 
 def per_device(stream_one, stream_two, stream_value, long_filter, short_taps, skip_gain, out_grad):
@@ -532,7 +564,8 @@
     def side_by_side(first, second):
         return jnp.concatenate([by_owner(first), by_owner(second)], 2)
 
-    steps = max(1, channels // 256)
+    small = pltpu.CompilerParams(vmem_limit_bytes=16 * 1024 * 1024)
+    steps = 2 if channels % 512 == 0 else 1
     by_columns = pl.BlockSpec((tokens, channels // steps), lambda i: (0, i))
 
     if exact:
@@ -566,7 +599,7 @@
     table_spec = pl.BlockSpec((1, tokens, 2 * size), lambda k: (k, 0, 0))
 
     if exact and blocks <= 16:
-        pieces = 4 if blocks % 4 == 0 else 1
+        group = 4
 
         def resident(*refs):
             resident_kernel(blocks, *refs)
@@ -574,16 +607,14 @@
         returned = pl.pallas_call(
             resident,
             out_shape=jax.ShapeDtypeStruct((blocks, rows_out, LANES), bf16),
-            in_specs=[ANY, VMEM, ANY, ANY],
-            out_specs=ANY,
+            in_specs=[VMEM, VMEM, HBM],
+            out_specs=VMEM,
             scratch_shapes=[
-                pltpu.VMEM((blocks, rows_in, LANES), bf16),
-                pltpu.VMEM((blocks + 1, size, 2 * size), bf16),
-                pltpu.VMEM((blocks + 1, size, 2 * size), bf16),
+                pltpu.VMEM((2, blocks + 1, tokens, 2 * size), bf16),
                 pltpu.VMEM((blocks + 1, size, 2 * LANES), bf16),
                 pltpu.VMEM((blocks + 1, size, 2 * LANES), bf16),
-                pltpu.VMEM((2, size, 2 * LANES), bf16),
-                pltpu.VMEM((2, size, 2 * LANES), bf16),
+                pltpu.VMEM((2 * group, size, 2 * LANES), bf16),
+                pltpu.VMEM((2 * group, size, 2 * LANES), bf16),
                 pltpu.VMEM((blocks + 1, size, 2 * LANES), f32),
                 pltpu.VMEM((blocks, tokens, LANES), f32),
                 pltpu.VMEM((blocks, tokens, LANES), f32),
@@ -591,19 +622,11 @@
                 pltpu.VMEM((blocks, tokens, LANES), f32),
                 pltpu.VMEM((blocks, half, LANES), f32),
                 pltpu.VMEM((8, 8, LANES), f32),
-                pltpu.VMEM((blocks, rows_out, LANES), bf16),
-                pltpu.SemaphoreType.DMA((pieces,)),
                 pltpu.SemaphoreType.DMA((2,)),
-                pltpu.SemaphoreType.DMA,
             ],
             compiler_params=pltpu.CompilerParams(vmem_limit_bytes=48 * 1024 * 1024),
             name="owner",
-        )(
-            owned_chunk,
-            weights,
-            jnp.asarray(full_tables(forward)),
-            jnp.asarray(full_tables(inverse)),
-        )
+        )(owned_chunk, weights, jnp.asarray(np.stack([forward, inverse])))
     else:
 
         def owner(*refs):
@@ -631,6 +654,16 @@
     if exact:
         shape = (tokens, channels)
         taps_spec = pl.BlockSpec((3, 3, channels // steps), lambda i: (0, 0, i))
+        gates_spec = pl.BlockSpec((3, tokens, channels // steps), lambda i: (0, 0, i))
+        gates = pl.pallas_call(
+            gates_kernel,
+            out_shape=jax.ShapeDtypeStruct((3,) + shape, f32),
+            grid=(steps,),
+            in_specs=[by_columns] * 3 + [taps_spec, ANY],
+            out_specs=gates_spec,
+            compiler_params=small,
+            name="gates",
+        )(stream_one, stream_two, stream_value, short_taps, returned)
         results = pl.pallas_call(
             finish_kernel,
             out_shape=[jax.ShapeDtypeStruct(shape, bf16)] * 4
@@ -639,22 +672,25 @@
                 jax.ShapeDtypeStruct(short_taps.shape, f32),
                 jax.ShapeDtypeStruct((1, channels), f32),
             ],
-            grid=(steps,),
-            in_specs=[by_columns] * 4
-            + [taps_spec, pl.BlockSpec((blocks // steps, rows_out, LANES), lambda i: (i, 0, 0))],
-            out_specs=[by_columns] * 5 + [taps_spec, pl.BlockSpec((1, channels // steps), lambda i: (0, i))],
+            in_specs=[VMEM] * 4,
+            out_specs=[ANY] * 5 + [VMEM] * 2,
+            scratch_shapes=[pltpu.VMEM(shape, bf16)] * 4
+            + [pltpu.VMEM(shape, f32), pltpu.SemaphoreType.DMA((5, 4))],
+            compiler_params=small,
             name="finish",
-        )(stream_one, stream_two, stream_value, out_grad, short_taps, back)
+        )(gates, out_grad, short_taps, back)
     else:
         wide = back.astype(f32)
 
         def joined(part):
             return part[:, :, :owned].transpose(1, 0, 2).reshape(rows_out, channels)
 
+        rows = [taps_flat[i : i + 1] for i in range(9)]
+        streams = [s.astype(f32) for s in (stream_one, stream_two, stream_value)]
         results = finish(
-            [s.astype(f32) for s in (stream_one, stream_two, stream_value)],
+            local_gates(streams, rows),
             out_grad.astype(f32),
-            [taps_flat[i : i + 1] for i in range(9)],
+            rows,
             joined(wide[:, :, :HALF]),
             joined(wide[:, :, HALF:]),
         )

time: 90.5 us -> 82.8 us (0.915)
  blocking collectives: 28 us -> 0 us
  waiting for transfers between devices: 29 us -> 48 us
  starting transfers between devices: 8.31 us -> 15.2 us
  Pallas kernels: 23.5 us -> 17.9 us
    all_to_all x1 -> x0, blocking collectives: 28 us -> none  [per_device(): back = lax.all_to_all(returned, 'seq', 0, 0, tiled=True)]
    all_to_all x0 -> x1, waiting for transfers between devices: none -> 19 us  [per_device(): back = lax.all_to_all(returned, 'seq', 0, 0, tiled=True)]
    all_to_all x0 -> x1, starting transfers between devices: none -> 6.71 us  [per_device(): back = lax.all_to_all(returned, 'seq', 0, 0, tiled=True)]
    pallas_call x1, Pallas kernels: 15.4 us -> 12 us  [per_device(): pl.pallas_call(resident, out_shape=jax.ShapeDtypeStruct((blocks, rows_out...]
    pallas_call x1, Pallas kernels: 4.33 us -> 2.52 us  [per_device(): pl.pallas_call(finish_kernel, out_shape=[jax.ShapeDtypeStruct(shape, bf16...]
    pallas_call x1, Pallas kernels: 3.74 us -> 2.62 us  [per_device(): pl.pallas_call(pack_kernel, out_shape=jax.ShapeDtypeStruct((blocks, rows_...]
  transfers between devices with their start and end apart: 1 -> 2, of which waited for: 1 -> 2; matrix products, arithmetic and copies ran while one was open for 0% -> 1% of each run, Pallas kernels for 0% -> 1%
where the time goes in v3:
time: 82.8 us; the launch traced here: 82.4 us
  waiting for transfers between devices  48 us (58%)
  Pallas kernels  17.9 us (22%)
  starting transfers between devices  15.2 us (18%)
    all_to_all x1, waiting for transfers between devices, per_device(): owned_chunk = lax.all_to_all(packed, 'seq', 0, 0, tiled=True)  29 us
    all_to_all x1, waiting for transfers between devices, per_device(): back = lax.all_to_all(returned, 'seq', 0, 0, tiled=True)  19 us
    pallas_call x1, Pallas kernels, per_device(): pl.pallas_call(resident, out_shape=jax.ShapeDtypeStruct((blocks, rows_out...  12 us
    all_to_all x1, starting transfers between devices, per_device(): owned_chunk = lax.all_to_all(packed, 'seq', 0, 0, tiled=True)  8.46 us
    all_to_all x1, starting transfers between devices, per_device(): back = lax.all_to_all(returned, 'seq', 0, 0, tiled=True)  6.71 us
    pallas_call x1, Pallas kernels, per_device(): pl.pallas_call(pack_kernel, out_shape=jax.ShapeDtypeStruct((blocks, rows_...  2.62 us
    pallas_call x1, Pallas kernels, per_device(): pl.pallas_call(finish_kernel, out_shape=[jax.ShapeDtypeStruct(shape, bf16...  2.52 us
  transfers between devices with their start and end apart: 2, of which 2 were waited for; matrix products, arithmetic and copies ran while one was open for 1% of the time, Pallas kernels for 1%

profile of v3, /device:TPU:0, one launch (start us, length us, event | category | flops | bytes accessed | tf_op | source)
XLA Modules:
  0.0 82.4 jit_solution(4182185096499804570)
XLA Ops:
  0.6 2.6 %pack.1 = bf16[16,320,128]{2,1,0:T(8,128)(2,1)} custom-call(bf16[128,1024]{1,0:T(8,128)(2,1)} %one.3, bf16[128,1024]{1,0:T(8,128)(2,1)} %two.3, bf16[128,1024]{1,0:T(8,128)(2,1)} %value.3, bf16[128,1024]{1,0:T(8,128)(2,1)} %filt.1, bf16[128,1024]{1,0:T(8,128)(2,1)} %grad.3), custom_call_target="tpu_custom_call" | custom-call | tf_op jit(solution)/shard_map/pack/pallas_call | solution.py:572
  3.3 0.0 copy-start.6
  3.3 0.0 slice-start
  3.3 0.0 slice-start.1
  3.3 0.0 copy-start.5
  3.3 8.5 %all-to-all-start = ((bf16[16,320,128]{2,1,0:T(8,128)(2,1)}), bf16[16,320,128]{2,1,0:T(8,128)(2,1)S(1)}, u32[]{:S(2)}, u32[]{:S(2)}) async-start(bf16[16,320,128]{2,1,0:T(8,128)(2,1)} %pack.1), calls=%async_computation | async-start | bytes 2621440 | tf_op jit(solution)/shard_map/all_to_all | solution.py:595
  11.7 0.0 copy-done.6
  11.8 0.1 concatenate.20
  11.8 0.0 slice-done
  11.8 0.1 concatenate.22
  11.9 0.0 slice-done.1
  12.0 0.1 concatenate.19
  12.1 0.0 copy-done.5
  12.1 0.1 fusion.3.refs_1_
  12.2 29.0 %all-to-all-done.refs_0_ = bf16[16,320,128]{2,1,0:T(8,128)(2,1)S(1)} async-done(((bf16[16,320,128]{2,1,0:T(8,128)(2,1)}), bf16[16,320,128]{2,1,0:T(8,128)(2,1)S(1)}, u32[]{:S(2)}, u32[]{:S(2)}) %all-to-all-start) | async-done | bytes 1310752 | tf_op jit(solution)/shard_map/all_to_all | solution.py:595
  41.2 12.0 %owner.1.after = bf16[16,208,128]{2,1,0:T(8,128)(2,1)} custom-call(bf16[16,320,128]{2,1,0:T(8,128)(2,1)S(1)} %all-to-all-done.refs_0_, f32[8,128]{1,0:T(8,128)S(1)} %fusion.3.refs_1_, bf16[2,17,128,512]{3,2,1,0:T(8,128)(2,1)} %constant.47.clone.refs_2_), custom_call_target="tpu_custom_call" | custom-call | tf_op jit(solution)/shard_map/owner/pallas_call | solution.py:607
  53.3 0.0 copy-start
  53.3 0.0 copy-start.1
  53.3 0.0 copy-start.2
  53.3 0.0 copy-start.4
  53.3 6.7 %all-to-all-start.1 = ((bf16[16,208,128]{2,1,0:T(8,128)(2,1)}), bf16[16,208,128]{2,1,0:T(8,128)(2,1)S(1)}, u32[]{:S(2)}, u32[]{:S(2)}) async-start(bf16[16,208,128]{2,1,0:T(8,128)(2,1)} %owner.1.after), calls=%async_computation.1 | async-start | bytes 1703936 | tf_op jit(solution)/shard_map/all_to_all | solution.py:652
  60.0 0.0 copy-done
  60.0 0.0 copy-done.1
  60.1 0.0 copy-done.2
  60.1 0.0 copy-done.4
  60.1 0.0 copy-start.3
  60.1 0.8 gates.1
  60.8 19.0 %all-to-all-done.1.back = bf16[16,208,128]{2,1,0:T(8,128)(2,1)S(1)} async-done(((bf16[16,208,128]{2,1,0:T(8,128)(2,1)}), bf16[16,208,128]{2,1,0:T(8,128)(2,1)S(1)}, u32[]{:S(2)}, u32[]{:S(2)}) %all-to-all-start.1) | async-done | bytes 852000 | tf_op jit(solution)/shard_map/all_to_all | solution.py:652
  79.9 0.0 copy-done.3
  79.9 2.5 %finish.1 = (bf16[128,1024]{1,0:T(8,128)(2,1)}, bf16[128,1024]{1,0:T(8,128)(2,1)}, bf16[128,1024]{1,0:T(8,128)(2,1)}, bf16[128,1024]{1,0:T(8,128)(2,1)}, f32[128...) custom-call(f32[3,128,1024]{2,1,0:T(8,128)S(1)} %gates.1, bf16[128,1024]{1,0:T(8,128)(2,1)S(1)} %copy-done.3, ...), custom_call_target="tpu_custom_call" | custom-call | tf_op jit(solution)/shard_map/finish/pallas_call | solution.py:667
  (3 shorter events, 0.1 us)
Async XLA Ops:
  3.3 8.5 %copy-start.6 = (f32[1024]{0:T(1024)S(1)}, f32[1024]{0:T(1024)}, u32[]{:S(2)}) copy-start(f32[1024]{0:T(1024)} %param.15) | copy-start | bytes 12292
  3.3 8.6 %slice-start = ((f32[3,3,1024]{2,1,0:T(4,128)}), f32[1,3,1024]{2,1,0:T(4,128)S(1)}, s32[]{:S(2)}) async-start(f32[3,3,1024]{2,1,0:T(4,128)} %weights.3), calls=%async_computation.2 | async-start | bytes 32768 | tf_op jit(solution)/shard_map/slice | solution.py:592
  3.3 8.7 %slice-start.1 = ((f32[3,3,1024]{2,1,0:T(4,128)}), f32[2,3,1024]{2,1,0:T(4,128)S(1)}, s32[]{:S(2)}) async-start(f32[3,3,1024]{2,1,0:T(4,128)} %weights.3), calls=%async_computation.3 | async-start | bytes 65536 | tf_op jit(solution)/shard_map/slice | solution.py:591
  3.3 8.8 %copy-start.5 = (f32[3,16,64]{2,0,1:T(4,128)S(1)}, f32[3,16,64]{2,0,1:T(4,128)}, u32[]{:S(2)}) copy-start(f32[3,16,64]{2,0,1:T(4,128)} %constant.42.clone.1) | copy-start | bytes 36868
  3.3 37.9 %all-to-all-start = ((bf16[16,320,128]{2,1,0:T(8,128)(2,1)}), bf16[16,320,128]{2,1,0:T(8,128)(2,1)S(1)}, u32[]{:S(2)}, u32[]{:S(2)}) async-start(bf16[16,320,128]{2,1,0:T(8,128)(2,1)} %pack.1), calls=%async_computation | async-start | bytes 2621440 | tf_op jit(solution)/shard_map/all_to_all | solution.py:595
  53.3 6.8 %copy-start = (bf16[128,1024]{1,0:T(8,128)(2,1)S(1)}, bf16[128,1024]{1,0:T(8,128)(2,1)}, u32[]{:S(2)}) copy-start(bf16[128,1024]{1,0:T(8,128)(2,1)} %one.3) | copy-start | bytes 786436
  53.3 6.8 %copy-start.1 = (bf16[128,1024]{1,0:T(8,128)(2,1)S(1)}, bf16[128,1024]{1,0:T(8,128)(2,1)}, u32[]{:S(2)}) copy-start(bf16[128,1024]{1,0:T(8,128)(2,1)} %two.3) | copy-start | bytes 786436
  53.3 6.8 %copy-start.2 = (bf16[128,1024]{1,0:T(8,128)(2,1)S(1)}, bf16[128,1024]{1,0:T(8,128)(2,1)}, u32[]{:S(2)}) copy-start(bf16[128,1024]{1,0:T(8,128)(2,1)} %value.3) | copy-start | bytes 786436
  53.3 6.8 %copy-start.4 = (f32[3,3,1024]{2,1,0:T(4,128)S(1)}, f32[3,3,1024]{2,1,0:T(4,128)}, u32[]{:S(2)}) copy-start(f32[3,3,1024]{2,1,0:T(4,128)} %weights.3) | copy-start | bytes 110596
  53.3 26.5 %all-to-all-start.1 = ((bf16[16,208,128]{2,1,0:T(8,128)(2,1)}), bf16[16,208,128]{2,1,0:T(8,128)(2,1)S(1)}, u32[]{:S(2)}, u32[]{:S(2)}) async-start(bf16[16,208,128]{2,1,0:T(8,128)(2,1)} %owner.1.after), calls=%async_computation.1 | async-start | bytes 1703936 | tf_op jit(solution)/shard_map/all_to_all | solution.py:652
  60.1 19.8 %copy-start.3 = (bf16[128,1024]{1,0:T(8,128)(2,1)S(1)}, bf16[128,1024]{1,0:T(8,128)(2,1)}, u32[]{:S(2)}) copy-start(bf16[128,1024]{1,0:T(8,128)(2,1)} %grad.3) | copy-start | bytes 786436

commit v4 on v3

--- a/solution.py
+++ b/solution.py
@@ -101,7 +101,7 @@
     half = tokens // 2
     for pair in range(one.shape[1] // LANES):
         cols = slice(pair * LANES, (pair + 1) * LANES)
-        tile = [ref[:, cols].astype(jnp.float32) for ref in (two, one, value, grad, filt)]
+        tile = [ref[:, cols] for ref in (two, one, value, grad, filt)]
         parts = (
             (0, tokens, tile[0], tile[1]),
             (tokens, tokens, tile[2], tile[3]),
@@ -306,7 +306,7 @@
 
     left, right = slice(0, LANES), slice(LANES, 2 * LANES)
 
-    @pl.loop(0, tokens // 16)
+    @pl.loop(0, tokens // 16, unroll=2)
     def _(r):
         at = pl.multiple_of(r * 16, 16)
         spectrum = padded_dft([ug_ref[a, pl.ds(at, 16)].astype(f32) for a in range(blocks)])
@@ -314,7 +314,7 @@
             put(k, at, left, real)
             put(k, tokens + at, left, jnp.zeros_like(real) if imag is None else imag)
 
-    @pl.loop(0, half // 16)
+    @pl.loop(0, half // 16, unroll=2)
     def _(r):
         at = pl.multiple_of(r * 16, 16)
         low = lax.broadcasted_iota(jnp.int32, (16, LANES), 1) < HALF
@@ -361,14 +361,14 @@
     def out_of_products(k, slot):
         spec_ref[k] = apply(1, k, zh_ref[slot], zl_ref[slot])
 
-    for copy in copies:
-        copy.wait()
+    copies[0].wait()
 
     group = zh_ref.shape[0] // 2
     whole = (blocks + 1) // group
     rest = range(whole * group, blocks + 1)
     for j in range(group):
         into_products(j, j)
+    copies[1].wait()
 
     @pl.loop(1, whole)
     def _(i):
@@ -402,7 +402,7 @@
             for a, total in enumerate(folded_sum(ys)):
                 lg_ref[a, pl.ds(row, 8)] = total + skip * ug[a][8 * sub : 8 * sub + 8]
 
-    @pl.loop(0, half // 8)
+    @pl.loop(0, half // 8, unroll=2)
     def _(r):
         at = pl.multiple_of(r * 8, 8)
         ys = []
@@ -425,7 +425,7 @@
             total = total + values[8 * r : 8 * r + 8]
         return total
 
-    @pl.loop(0, blocks)
+    @pl.loop(0, blocks, unroll=4)
     def _(i):
         a = blocks - 1 - i
         one, two = window(a, 0), window(a, tokens)
@@ -448,7 +448,7 @@
     sums[3] = jnp.where(lower, sums[3], halves_swapped(gf_ref[0, :8])[:1])
     tail = jnp.concatenate(sums + [jnp.zeros((2, LANES), f32)], 0)
 
-    @pl.loop(0, blocks)
+    @pl.loop(0, blocks, unroll=4)
     def _(a):
         rows = out[a, tokens + half :].astype(f32)
         out[a, tokens + half :] = jnp.concatenate([rows[:8], tail], 0).astype(out.dtype)
@@ -599,7 +599,7 @@
     table_spec = pl.BlockSpec((1, tokens, 2 * size), lambda k: (k, 0, 0))
 
     if exact and blocks <= 16:
-        group = 4
+        group = 6
 
         def resident(*refs):
             resident_kernel(blocks, *refs)

time: 82.8 us -> 80.6 us (0.973)
  Pallas kernels: 17.9 us -> 15.8 us
    pallas_call x1, Pallas kernels: 12 us -> 9.99 us  [per_device(): pl.pallas_call(resident, out_shape=jax.ShapeDtypeStruct((blocks, rows_out...]
where the time goes in v4:
time: 80.6 us; the launch traced here: 80.3 us
  waiting for transfers between devices  48 us (60%)
  Pallas kernels  15.8 us (20%)
  starting transfers between devices  15.2 us (19%)
    all_to_all x1, waiting for transfers between devices, per_device(): owned_chunk = lax.all_to_all(packed, 'seq', 0, 0, tiled=True)  29 us
    all_to_all x1, waiting for transfers between devices, per_device(): back = lax.all_to_all(returned, 'seq', 0, 0, tiled=True)  19 us
    pallas_call x1, Pallas kernels, per_device(): pl.pallas_call(resident, out_shape=jax.ShapeDtypeStruct((blocks, rows_out...  9.99 us
    all_to_all x1, starting transfers between devices, per_device(): owned_chunk = lax.all_to_all(packed, 'seq', 0, 0, tiled=True)  8.46 us
    all_to_all x1, starting transfers between devices, per_device(): back = lax.all_to_all(returned, 'seq', 0, 0, tiled=True)  6.71 us
    pallas_call x1, Pallas kernels, per_device(): pl.pallas_call(pack_kernel, out_shape=jax.ShapeDtypeStruct((blocks, rows_...  2.55 us
    pallas_call x1, Pallas kernels, per_device(): pl.pallas_call(finish_kernel, out_shape=[jax.ShapeDtypeStruct(shape, bf16...  2.52 us
  transfers between devices with their start and end apart: 2, of which 2 were waited for; matrix products, arithmetic and copies ran while one was open for 1% of the time, Pallas kernels for 1%

profile of v4, /device:TPU:0, one launch (start us, length us, event | category | flops | bytes accessed | tf_op | source)
XLA Modules:
  0.0 80.3 jit_solution(17723472975180097775)
XLA Ops:
  0.6 2.6 %pack.1 = bf16[16,320,128]{2,1,0:T(8,128)(2,1)} custom-call(bf16[128,1024]{1,0:T(8,128)(2,1)} %one.3, bf16[128,1024]{1,0:T(8,128)(2,1)} %two.3, bf16[128,1024]{1,0:T(8,128)(2,1)} %value.3, bf16[128,1024]{1,0:T(8,128)(2,1)} %filt.1, bf16[128,1024]{1,0:T(8,128)(2,1)} %grad.3), custom_call_target="tpu_custom_call" | custom-call | tf_op jit(solution)/shard_map/pack/pallas_call | solution.py:572
  3.2 0.0 copy-start.6
  3.2 0.0 slice-start
  3.2 0.0 slice-start.1
  3.2 0.0 copy-start.5
  3.2 8.5 %all-to-all-start = ((bf16[16,320,128]{2,1,0:T(8,128)(2,1)}), bf16[16,320,128]{2,1,0:T(8,128)(2,1)S(1)}, u32[]{:S(2)}, u32[]{:S(2)}) async-start(bf16[16,320,128]{2,1,0:T(8,128)(2,1)} %pack.1), calls=%async_computation | async-start | bytes 2621440 | tf_op jit(solution)/shard_map/all_to_all | solution.py:595
  11.7 0.0 copy-done.6
  11.7 0.1 concatenate.20
  11.8 0.0 slice-done
  11.8 0.1 concatenate.22
  11.9 0.0 slice-done.1
  11.9 0.1 concatenate.19
  12.0 0.0 copy-done.5
  12.1 0.1 fusion.3.refs_1_
  12.1 29.0 %all-to-all-done.refs_0_ = bf16[16,320,128]{2,1,0:T(8,128)(2,1)S(1)} async-done(((bf16[16,320,128]{2,1,0:T(8,128)(2,1)}), bf16[16,320,128]{2,1,0:T(8,128)(2,1)S(1)}, u32[]{:S(2)}, u32[]{:S(2)}) %all-to-all-start) | async-done | bytes 1310752 | tf_op jit(solution)/shard_map/all_to_all | solution.py:595
  41.2 10.0 %owner.1.after = bf16[16,208,128]{2,1,0:T(8,128)(2,1)} custom-call(bf16[16,320,128]{2,1,0:T(8,128)(2,1)S(1)} %all-to-all-done.refs_0_, f32[8,128]{1,0:T(8,128)S(1)} %fusion.3.refs_1_, bf16[2,17,128,512]{3,2,1,0:T(8,128)(2,1)} %constant.47.clone.refs_2_), custom_call_target="tpu_custom_call" | custom-call | tf_op jit(solution)/shard_map/owner/pallas_call | solution.py:607
  51.1 0.0 copy-start
  51.2 0.0 copy-start.1
  51.2 0.0 copy-start.2
  51.2 0.0 copy-start.4
  51.2 6.7 %all-to-all-start.1 = ((bf16[16,208,128]{2,1,0:T(8,128)(2,1)}), bf16[16,208,128]{2,1,0:T(8,128)(2,1)S(1)}, u32[]{:S(2)}, u32[]{:S(2)}) async-start(bf16[16,208,128]{2,1,0:T(8,128)(2,1)} %owner.1.after), calls=%async_computation.1 | async-start | bytes 1703936 | tf_op jit(solution)/shard_map/all_to_all | solution.py:652
  57.9 0.0 copy-done
  57.9 0.0 copy-done.1
  57.9 0.0 copy-done.2
  57.9 0.0 copy-done.4
  58.0 0.0 copy-start.3
  58.0 0.8 gates.1
  58.7 19.0 %all-to-all-done.1.back = bf16[16,208,128]{2,1,0:T(8,128)(2,1)S(1)} async-done(((bf16[16,208,128]{2,1,0:T(8,128)(2,1)}), bf16[16,208,128]{2,1,0:T(8,128)(2,1)S(1)}, u32[]{:S(2)}, u32[]{:S(2)}) %all-to-all-start.1) | async-done | bytes 852000 | tf_op jit(solution)/shard_map/all_to_all | solution.py:652
  77.7 0.0 copy-done.3
  77.7 2.5 %finish.1 = (bf16[128,1024]{1,0:T(8,128)(2,1)}, bf16[128,1024]{1,0:T(8,128)(2,1)}, bf16[128,1024]{1,0:T(8,128)(2,1)}, bf16[128,1024]{1,0:T(8,128)(2,1)}, f32[128...) custom-call(f32[3,128,1024]{2,1,0:T(8,128)S(1)} %gates.1, bf16[128,1024]{1,0:T(8,128)(2,1)S(1)} %copy-done.3, ...), custom_call_target="tpu_custom_call" | custom-call | tf_op jit(solution)/shard_map/finish/pallas_call | solution.py:667
  (3 shorter events, 0.1 us)
Async XLA Ops:
  3.2 8.5 %copy-start.6 = (f32[1024]{0:T(1024)S(1)}, f32[1024]{0:T(1024)}, u32[]{:S(2)}) copy-start(f32[1024]{0:T(1024)} %param.15) | copy-start | bytes 12292
  3.2 8.6 %slice-start = ((f32[3,3,1024]{2,1,0:T(4,128)}), f32[1,3,1024]{2,1,0:T(4,128)S(1)}, s32[]{:S(2)}) async-start(f32[3,3,1024]{2,1,0:T(4,128)} %weights.3), calls=%async_computation.2 | async-start | bytes 32768 | tf_op jit(solution)/shard_map/slice | solution.py:592
  3.2 8.7 %slice-start.1 = ((f32[3,3,1024]{2,1,0:T(4,128)}), f32[2,3,1024]{2,1,0:T(4,128)S(1)}, s32[]{:S(2)}) async-start(f32[3,3,1024]{2,1,0:T(4,128)} %weights.3), calls=%async_computation.3 | async-start | bytes 65536 | tf_op jit(solution)/shard_map/slice | solution.py:591
  3.2 8.8 %copy-start.5 = (f32[3,16,64]{2,0,1:T(4,128)S(1)}, f32[3,16,64]{2,0,1:T(4,128)}, u32[]{:S(2)}) copy-start(f32[3,16,64]{2,0,1:T(4,128)} %constant.42.clone.1) | copy-start | bytes 36868
  3.2 37.9 %all-to-all-start = ((bf16[16,320,128]{2,1,0:T(8,128)(2,1)}), bf16[16,320,128]{2,1,0:T(8,128)(2,1)S(1)}, u32[]{:S(2)}, u32[]{:S(2)}) async-start(bf16[16,320,128]{2,1,0:T(8,128)(2,1)} %pack.1), calls=%async_computation | async-start | bytes 2621440 | tf_op jit(solution)/shard_map/all_to_all | solution.py:595
  51.1 6.8 %copy-start = (bf16[128,1024]{1,0:T(8,128)(2,1)S(1)}, bf16[128,1024]{1,0:T(8,128)(2,1)}, u32[]{:S(2)}) copy-start(bf16[128,1024]{1,0:T(8,128)(2,1)} %one.3) | copy-start | bytes 786436
  51.2 6.8 %copy-start.1 = (bf16[128,1024]{1,0:T(8,128)(2,1)S(1)}, bf16[128,1024]{1,0:T(8,128)(2,1)}, u32[]{:S(2)}) copy-start(bf16[128,1024]{1,0:T(8,128)(2,1)} %two.3) | copy-start | bytes 786436
  51.2 6.8 %copy-start.2 = (bf16[128,1024]{1,0:T(8,128)(2,1)S(1)}, bf16[128,1024]{1,0:T(8,128)(2,1)}, u32[]{:S(2)}) copy-start(bf16[128,1024]{1,0:T(8,128)(2,1)} %value.3) | copy-start | bytes 786436
  51.2 6.8 %copy-start.4 = (f32[3,3,1024]{2,1,0:T(4,128)S(1)}, f32[3,3,1024]{2,1,0:T(4,128)}, u32[]{:S(2)}) copy-start(f32[3,3,1024]{2,1,0:T(4,128)} %weights.3) | copy-start | bytes 110596
  51.2 26.5 %all-to-all-start.1 = ((bf16[16,208,128]{2,1,0:T(8,128)(2,1)}), bf16[16,208,128]{2,1,0:T(8,128)(2,1)S(1)}, u32[]{:S(2)}, u32[]{:S(2)}) async-start(bf16[16,208,128]{2,1,0:T(8,128)(2,1)} %owner.1.after), calls=%async_computation.1 | async-start | bytes 1703936 | tf_op jit(solution)/shard_map/all_to_all | solution.py:652
  58.0 19.8 %copy-start.3 = (bf16[128,1024]{1,0:T(8,128)(2,1)S(1)}, bf16[128,1024]{1,0:T(8,128)(2,1)}, u32[]{:S(2)}) copy-start(bf16[128,1024]{1,0:T(8,128)(2,1)} %grad.3) | copy-start | bytes 786436

commit v5 on v4

--- a/solution.py
+++ b/solution.py
@@ -272,7 +272,7 @@
 def resident_kernel(
     blocks, chunk, weights, tables_hbm, out,
     tables, high_ref, low_ref, zh_ref, zl_ref, spec_ref,
-    c1_ref, c2_ref, ug_ref, lg_ref, gf_ref, acc_ref, sems,
+    s1_ref, s2_ref, c1_ref, c2_ref, ug_ref, lg_ref, gf_ref, acc_ref, sems,
 ):
     tokens = tables.shape[2]
     size = 2 * tokens
@@ -284,18 +284,24 @@
     for copy in copies:
         copy.start()
 
-    def window(a, start):
-        before = chunk[jnp.maximum(a - 1, 0), start + tokens - 16 : start + tokens].astype(f32)[8:]
-        body = chunk[a, start : start + tokens].astype(f32)
-        return jnp.concatenate([jnp.where(a > 0, before, 0.0), body], axis=0)
-
     w1 = [weights[j : j + 1] for j in range(3)]
     w2 = [weights[3 + j : 4 + j] for j in range(3)]
 
+    s1_ref[:8] = jnp.zeros((8, LANES), f32)
+    s2_ref[:8] = jnp.zeros((8, LANES), f32)
+
+    def earlier(ref, a, j):
+        return ref[pl.ds(a * tokens + (8 - j), tokens)]
+
+    def conv(ref, a, own, w):
+        return w[0] * own + w[1] * earlier(ref, a, 1) + w[2] * earlier(ref, a, 2)
+
     @pl.loop(0, blocks)
     def _(a):
-        c1 = window_conv(window(a, 0), w1, tokens)
-        c2 = window_conv(window(a, tokens), w2, tokens)
+        at = pl.multiple_of(a * tokens + 8, 8)
+        one, two = chunk[a, :tokens].astype(f32), chunk[a, tokens : 2 * tokens].astype(f32)
+        s1_ref[pl.ds(at, tokens)], s2_ref[pl.ds(at, tokens)] = one, two
+        c1, c2 = conv(s1_ref, a, one, w1), conv(s2_ref, a, two, w2)
         c1_ref[a], c2_ref[a] = c1, c2
         ug_ref[a] = (c1 * c2).astype(bf16)
 
@@ -428,18 +434,18 @@
     @pl.loop(0, blocks, unroll=4)
     def _(i):
         a = blocks - 1 - i
-        one, two = window(a, 0), window(a, tokens)
         lg = lg_ref[a]
         turned = halves_swapped(lg)
         x1, x2 = c2_ref[a] * turned, c1_ref[a] * turned
         for j in range(3):
-            acc_ref[j] += folded(x1 * one[8 - j : 8 - j + tokens])
-            acc_ref[3 + j] += folded(x2 * two[8 - j : 8 - j + tokens])
+            acc_ref[j] += folded(x1 * earlier(s1_ref, a, j))
+            acc_ref[3 + j] += folded(x2 * earlier(s2_ref, a, j))
         after = acc_ref[7]
+        before = pl.multiple_of(a * tokens, 8)
         out[a, :tokens] = lg.astype(out.dtype)
         out[a, tokens : tokens + half] = gf_ref[a].astype(out.dtype)
         out[a, tokens + half :] = jnp.concatenate(
-            [after[:4], one[6:8], two[6:8], jnp.zeros((8, LANES), f32)], 0
+            [after[:4], s1_ref[pl.ds(before, 8)][6:], s2_ref[pl.ds(before, 8)][6:], jnp.zeros((8, LANES), f32)], 0
         ).astype(out.dtype)
         acc_ref[7] = jnp.concatenate([x1[:2], x2[:2], jnp.zeros((4, LANES), f32)], 0)
 
@@ -488,8 +494,11 @@
         for j in (1, 2):
             total = total + weights[3 * s + j] * trailing[j : j + tokens]
         grads.append(total)
-    taps = [high[at + 8 : at + 11], low[at + 8 : at + 11], low[at + 11 : at + 14]]
-    return [mixed_out] + grads + [grad_filter] + taps + [high[at + 11 : at + 12]]
+    return [mixed_out] + grads + [grad_filter]
+
+
+def token_sums(low, high):
+    return [high[:3], low[:3], low[3:6], high[3:4]]
 
 
 def gates_kernel(one, two, value, weights, after, gates):
@@ -505,14 +514,27 @@
 
 
 def finish_kernel(gates, grad, weights, back, *refs):
-    targets, grad_taps, grad_skip = refs[:5], refs[5], refs[6]
-    buffers, sems = refs[7:12], refs[12]
+    targets, buffers, sems, sum_sems = refs[:7], refs[7:14], refs[14], refs[15]
+    grad_taps, grad_skip = buffers[5:]
     pieces = sems.shape[1]
     width = grad.shape[1] // pieces
 
     def copy(i, piece):
         cols = pl.ds(piece * width, width)
         return pltpu.make_async_copy(buffers[i].at[:, cols], targets[i].at[:, cols], sems.at[i, piece])
+
+    for owner in range(0, back.shape[0], 2):
+        cols = slice(owner * HALF, (owner + 2) * HALF)
+        last = [back[owner + side, -16:].astype(jnp.float32)[8:] for side in range(2)]
+        totals = token_sums(*interleave(*last))
+        for s in range(3):
+            grad_taps[s, :, cols] = totals[s]
+        grad_skip[:, cols] = totals[3]
+    sum_copies = [
+        pltpu.make_async_copy(buffers[5 + i], targets[5 + i], sum_sems.at[i]) for i in range(2)
+    ]
+    for small_copy in sum_copies:
+        small_copy.start()
 
     for piece in range(pieces):
         for start in range(piece * width, (piece + 1) * width, LANES):
@@ -530,14 +552,13 @@
             )
             for ref, result in zip(buffers, results[:5]):
                 ref[:, cols] = result.astype(ref.dtype)
-            for s in range(3):
-                grad_taps[s, :, cols] = results[5 + s]
-            grad_skip[:, cols] = results[8]
         for i in range(5):
             copy(i, piece).start()
     for piece in range(pieces):
         for i in range(5):
             copy(i, piece).wait()
+    for small_copy in sum_copies:
+        small_copy.wait()
 
 
 VMEM = pl.BlockSpec(memory_space=pltpu.VMEM)
@@ -616,6 +637,8 @@
                 pltpu.VMEM((2 * group, size, 2 * LANES), bf16),
                 pltpu.VMEM((2 * group, size, 2 * LANES), bf16),
                 pltpu.VMEM((blocks + 1, size, 2 * LANES), f32),
+                pltpu.VMEM((blocks * tokens + 8, LANES), f32),
+                pltpu.VMEM((blocks * tokens + 8, LANES), f32),
                 pltpu.VMEM((blocks, tokens, LANES), f32),
                 pltpu.VMEM((blocks, tokens, LANES), f32),
                 pltpu.VMEM((blocks, tokens, LANES), bf16),
@@ -673,9 +696,15 @@
                 jax.ShapeDtypeStruct((1, channels), f32),
             ],
             in_specs=[VMEM] * 4,
-            out_specs=[ANY] * 5 + [VMEM] * 2,
+            out_specs=[ANY] * 7,
             scratch_shapes=[pltpu.VMEM(shape, bf16)] * 4
-            + [pltpu.VMEM(shape, f32), pltpu.SemaphoreType.DMA((5, 4))],
+            + [
+                pltpu.VMEM(shape, f32),
+                pltpu.VMEM(short_taps.shape, f32),
+                pltpu.VMEM((1, channels), f32),
+                pltpu.SemaphoreType.DMA((5, 4)),
+                pltpu.SemaphoreType.DMA((2,)),
+            ],
             compiler_params=small,
             name="finish",
         )(gates, out_grad, short_taps, back)
@@ -685,19 +714,15 @@
         def joined(part):
             return part[:, :, :owned].transpose(1, 0, 2).reshape(rows_out, channels)
 
+        low, high = joined(wide[:, :, :HALF]), joined(wide[:, :, HALF:])
         rows = [taps_flat[i : i + 1] for i in range(9)]
         streams = [s.astype(f32) for s in (stream_one, stream_two, stream_value)]
-        results = finish(
-            local_gates(streams, rows),
-            out_grad.astype(f32),
-            rows,
-            joined(wide[:, :, :HALF]),
-            joined(wide[:, :, HALF:]),
-        )
+        results = finish(local_gates(streams, rows), out_grad.astype(f32), rows, low, high)
+        totals = token_sums(low[-8:], high[-8:])
         results = [r.astype(bf16) for r in results[:4]] + [
             results[4],
-            jnp.stack(results[5:8]),
-            results[8],
+            jnp.stack(totals[:3]),
+            totals[3],
         ]
     return tuple(results[:6]) + (results[6].reshape(channels),)
 

time: 80.6 us -> 79.9 us (level)
  no operation moved by 1% of the time
where the time goes in v5:
time: 79.9 us; the launch traced here: 79.5 us
  waiting for transfers between devices  48 us (60%)
  starting transfers between devices  15.2 us (19%)
  Pallas kernels  15 us (19%)
  between operations  0.8 us (1%)
    all_to_all x1, waiting for transfers between devices, per_device(): owned_chunk = lax.all_to_all(packed, 'seq', 0, 0, tiled=True)  29 us
    all_to_all x1, waiting for transfers between devices, per_device(): back = lax.all_to_all(returned, 'seq', 0, 0, tiled=True)  19 us
    pallas_call x1, Pallas kernels, per_device(): pl.pallas_call(resident, out_shape=jax.ShapeDtypeStruct((blocks, rows_out...  9.82 us
    all_to_all x1, starting transfers between devices, per_device(): owned_chunk = lax.all_to_all(packed, 'seq', 0, 0, tiled=True)  8.46 us
    all_to_all x1, starting transfers between devices, per_device(): back = lax.all_to_all(returned, 'seq', 0, 0, tiled=True)  6.71 us
    pallas_call x1, Pallas kernels, per_device(): pl.pallas_call(pack_kernel, out_shape=jax.ShapeDtypeStruct((blocks, rows_...  2.55 us
    pallas_call x1, Pallas kernels, per_device(): pl.pallas_call(finish_kernel, out_shape=[jax.ShapeDtypeStruct(shape, bf16...  1.91 us
  transfers between devices with their start and end apart: 2, of which 2 were waited for; matrix products, arithmetic and copies ran while one was open for 1% of the time, Pallas kernels for 1%

profile of v5, /device:TPU:0, one launch (start us, length us, event | category | flops | bytes accessed | tf_op | source)
XLA Modules:
  0.0 79.5 jit_solution(6838317565117755714)
XLA Ops:
  0.6 2.6 %pack.1 = bf16[16,320,128]{2,1,0:T(8,128)(2,1)} custom-call(bf16[128,1024]{1,0:T(8,128)(2,1)} %one.3, bf16[128,1024]{1,0:T(8,128)(2,1)} %two.3, bf16[128,1024]{1,0:T(8,128)(2,1)} %value.3, bf16[128,1024]{1,0:T(8,128)(2,1)} %filt.1, bf16[128,1024]{1,0:T(8,128)(2,1)} %grad.3), custom_call_target="tpu_custom_call" | custom-call | tf_op jit(solution)/shard_map/pack/pallas_call | solution.py:593
  3.2 0.0 copy-start.6
  3.2 0.0 slice-start
  3.2 0.0 slice-start.1
  3.2 0.0 copy-start.5
  3.2 8.5 %all-to-all-start = ((bf16[16,320,128]{2,1,0:T(8,128)(2,1)}), bf16[16,320,128]{2,1,0:T(8,128)(2,1)S(1)}, u32[]{:S(2)}, u32[]{:S(2)}) async-start(bf16[16,320,128]{2,1,0:T(8,128)(2,1)} %pack.1), calls=%async_computation | async-start | bytes 2621440 | tf_op jit(solution)/shard_map/all_to_all | solution.py:616
  11.7 0.0 copy-done.6
  11.7 0.1 concatenate.20
  11.8 0.0 slice-done
  11.8 0.1 concatenate.22
  11.9 0.0 slice-done.1
  11.9 0.1 concatenate.19
  12.0 0.0 copy-done.5
  12.1 0.1 fusion.3.refs_1_
  12.1 29.0 %all-to-all-done.refs_0_ = bf16[16,320,128]{2,1,0:T(8,128)(2,1)S(1)} async-done(((bf16[16,320,128]{2,1,0:T(8,128)(2,1)}), bf16[16,320,128]{2,1,0:T(8,128)(2,1)S(1)}, u32[]{:S(2)}, u32[]{:S(2)}) %all-to-all-start) | async-done | bytes 1310752 | tf_op jit(solution)/shard_map/all_to_all | solution.py:616
  41.2 9.8 %owner.1.after = bf16[16,208,128]{2,1,0:T(8,128)(2,1)} custom-call(bf16[16,320,128]{2,1,0:T(8,128)(2,1)S(1)} %all-to-all-done.refs_0_, f32[8,128]{1,0:T(8,128)S(1)} %fusion.3.refs_1_, bf16[2,17,128,512]{3,2,1,0:T(8,128)(2,1)} %constant.47.clone.refs_2_), custom_call_target="tpu_custom_call" | custom-call | tf_op jit(solution)/shard_map/owner/pallas_call | solution.py:628
  51.0 0.0 copy-start
  51.0 0.0 copy-start.1
  51.0 0.0 copy-start.2
  51.0 0.0 copy-start.4
  51.0 6.7 %all-to-all-start.1 = ((bf16[16,208,128]{2,1,0:T(8,128)(2,1)}), bf16[16,208,128]{2,1,0:T(8,128)(2,1)S(1)}, u32[]{:S(2)}, u32[]{:S(2)}) async-start(bf16[16,208,128]{2,1,0:T(8,128)(2,1)} %owner.1.after), calls=%async_computation.1 | async-start | bytes 1703936 | tf_op jit(solution)/shard_map/all_to_all | solution.py:675
  57.7 0.0 copy-done
  57.8 0.0 copy-done.1
  57.8 0.0 copy-done.2
  57.8 0.0 copy-done.4
  57.8 0.0 copy-start.3
  57.8 0.8 gates.1
  58.6 19.0 %all-to-all-done.1.back = bf16[16,208,128]{2,1,0:T(8,128)(2,1)S(1)} async-done(((bf16[16,208,128]{2,1,0:T(8,128)(2,1)}), bf16[16,208,128]{2,1,0:T(8,128)(2,1)S(1)}, u32[]{:S(2)}, u32[]{:S(2)}) %all-to-all-start.1) | async-done | bytes 852000 | tf_op jit(solution)/shard_map/all_to_all | solution.py:675
  77.6 0.0 copy-done.3
  77.6 1.9 %finish.1 = (bf16[128,1024]{1,0:T(8,128)(2,1)}, bf16[128,1024]{1,0:T(8,128)(2,1)}, bf16[128,1024]{1,0:T(8,128)(2,1)}, bf16[128,1024]{1,0:T(8,128)(2,1)}, f32[128...) custom-call(f32[3,128,1024]{2,1,0:T(8,128)S(1)} %gates.1, bf16[128,1024]{1,0:T(8,128)(2,1)S(1)} %copy-done.3, ...), custom_call_target="tpu_custom_call" | custom-call | tf_op jit(solution)/shard_map/finish/pallas_call | solution.py:690
  (3 shorter events, 0.1 us)
Async XLA Ops:
  3.2 8.5 %copy-start.6 = (f32[1024]{0:T(1024)S(1)}, f32[1024]{0:T(1024)}, u32[]{:S(2)}) copy-start(f32[1024]{0:T(1024)} %param.15) | copy-start | bytes 12292
  3.2 8.6 %slice-start = ((f32[3,3,1024]{2,1,0:T(4,128)}), f32[1,3,1024]{2,1,0:T(4,128)S(1)}, s32[]{:S(2)}) async-start(f32[3,3,1024]{2,1,0:T(4,128)} %weights.3), calls=%async_computation.2 | async-start | bytes 32768 | tf_op jit(solution)/shard_map/slice | solution.py:613
  3.2 8.7 %slice-start.1 = ((f32[3,3,1024]{2,1,0:T(4,128)}), f32[2,3,1024]{2,1,0:T(4,128)S(1)}, s32[]{:S(2)}) async-start(f32[3,3,1024]{2,1,0:T(4,128)} %weights.3), calls=%async_computation.3 | async-start | bytes 65536 | tf_op jit(solution)/shard_map/slice | solution.py:612
  3.2 8.8 %copy-start.5 = (f32[3,16,64]{2,0,1:T(4,128)S(1)}, f32[3,16,64]{2,0,1:T(4,128)}, u32[]{:S(2)}) copy-start(f32[3,16,64]{2,0,1:T(4,128)} %constant.42.clone.1) | copy-start | bytes 36868
  3.2 37.9 %all-to-all-start = ((bf16[16,320,128]{2,1,0:T(8,128)(2,1)}), bf16[16,320,128]{2,1,0:T(8,128)(2,1)S(1)}, u32[]{:S(2)}, u32[]{:S(2)}) async-start(bf16[16,320,128]{2,1,0:T(8,128)(2,1)} %pack.1), calls=%async_computation | async-start | bytes 2621440 | tf_op jit(solution)/shard_map/all_to_all | solution.py:616
  51.0 6.8 %copy-start = (bf16[128,1024]{1,0:T(8,128)(2,1)S(1)}, bf16[128,1024]{1,0:T(8,128)(2,1)}, u32[]{:S(2)}) copy-start(bf16[128,1024]{1,0:T(8,128)(2,1)} %one.3) | copy-start | bytes 786436
  51.0 6.8 %copy-start.1 = (bf16[128,1024]{1,0:T(8,128)(2,1)S(1)}, bf16[128,1024]{1,0:T(8,128)(2,1)}, u32[]{:S(2)}) copy-start(bf16[128,1024]{1,0:T(8,128)(2,1)} %two.3) | copy-start | bytes 786436
  51.0 6.8 %copy-start.2 = (bf16[128,1024]{1,0:T(8,128)(2,1)S(1)}, bf16[128,1024]{1,0:T(8,128)(2,1)}, u32[]{:S(2)}) copy-start(bf16[128,1024]{1,0:T(8,128)(2,1)} %value.3) | copy-start | bytes 786436
  51.0 6.8 %copy-start.4 = (f32[3,3,1024]{2,1,0:T(4,128)S(1)}, f32[3,3,1024]{2,1,0:T(4,128)}, u32[]{:S(2)}) copy-start(f32[3,3,1024]{2,1,0:T(4,128)} %weights.3) | copy-start | bytes 110596
  51.0 26.5 %all-to-all-start.1 = ((bf16[16,208,128]{2,1,0:T(8,128)(2,1)}), bf16[16,208,128]{2,1,0:T(8,128)(2,1)S(1)}, u32[]{:S(2)}, u32[]{:S(2)}) async-start(bf16[16,208,128]{2,1,0:T(8,128)(2,1)} %owner.1.after), calls=%async_computation.1 | async-start | bytes 1703936 | tf_op jit(solution)/shard_map/all_to_all | solution.py:675
  57.8 19.8 %copy-start.3 = (bf16[128,1024]{1,0:T(8,128)(2,1)S(1)}, bf16[128,1024]{1,0:T(8,128)(2,1)}, u32[]{:S(2)}) copy-start(bf16[128,1024]{1,0:T(8,128)(2,1)} %grad.3) | copy-start | bytes 786436

commit v6 on v5

--- a/solution.py
+++ b/solution.py
@@ -296,14 +296,25 @@
     def conv(ref, a, own, w):
         return w[0] * own + w[1] * earlier(ref, a, 1) + w[2] * earlier(ref, a, 2)
 
-    @pl.loop(0, blocks)
+    acc_ref[...] = jnp.zeros_like(acc_ref)
+
+    def folded(values):
+        rows = [values[r : r + 8] for r in range(0, tokens, 8)]
+        while len(rows) > 1:
+            rows = [sum(rows[r : r + 2]) for r in range(0, len(rows), 2)]
+        return rows[0]
+
+    @pl.loop(0, blocks, unroll=blocks)
     def _(a):
         at = pl.multiple_of(a * tokens + 8, 8)
         one, two = chunk[a, :tokens].astype(f32), chunk[a, tokens : 2 * tokens].astype(f32)
         s1_ref[pl.ds(at, tokens)], s2_ref[pl.ds(at, tokens)] = one, two
         c1, c2 = conv(s1_ref, a, one, w1), conv(s2_ref, a, two, w2)
         c1_ref[a], c2_ref[a] = c1, c2
-        ug_ref[a] = (c1 * c2).astype(bf16)
+        ug = (c1 * c2).astype(bf16)
+        ug_ref[a] = ug
+        ug = ug.astype(f32)
+        acc_ref[6] += folded(ug * halves_swapped(ug))
 
     def put(k, row, cols, values):
         high = values.astype(bf16)
@@ -395,7 +406,7 @@
     skip = weights[6:7]
     low8 = lax.broadcasted_iota(jnp.int32, (8, LANES), 1) < HALF
 
-    @pl.loop(0, tokens // 16)
+    @pl.loop(0, tokens // 16, unroll=tokens // 16)
     def _(r):
         at = pl.multiple_of(r * 16, 16)
         ug = [ug_ref[a, pl.ds(at, 16)].astype(f32) for a in range(blocks)]
@@ -408,7 +419,7 @@
             for a, total in enumerate(folded_sum(ys)):
                 lg_ref[a, pl.ds(row, 8)] = total + skip * ug[a][8 * sub : 8 * sub + 8]
 
-    @pl.loop(0, half // 8, unroll=2)
+    @pl.loop(0, half // 8, unroll=half // 8)
     def _(r):
         at = pl.multiple_of(r * 8, 8)
         ys = []
@@ -423,15 +434,7 @@
         for a, total in enumerate(folded_sum(ys)):
             gf_ref[a, pl.ds(at, 8)] = total
 
-    acc_ref[...] = jnp.zeros_like(acc_ref)
-
-    def folded(values):
-        total = values[:8]
-        for r in range(1, tokens // 8):
-            total = total + values[8 * r : 8 * r + 8]
-        return total
-
-    @pl.loop(0, blocks, unroll=4)
+    @pl.loop(0, blocks, unroll=blocks)
     def _(i):
         a = blocks - 1 - i
         lg = lg_ref[a]
@@ -450,11 +453,11 @@
         acc_ref[7] = jnp.concatenate([x1[:2], x2[:2], jnp.zeros((4, LANES), f32)], 0)
 
     lower = lax.broadcasted_iota(jnp.int32, (1, LANES), 1) < HALF
-    sums = [jnp.sum(acc_ref[j], axis=0, keepdims=True) for j in range(6)]
-    sums[3] = jnp.where(lower, sums[3], halves_swapped(gf_ref[0, :8])[:1])
-    tail = jnp.concatenate(sums + [jnp.zeros((2, LANES), f32)], 0)
-
-    @pl.loop(0, blocks, unroll=4)
+    sums = [jnp.sum(acc_ref[j], axis=0, keepdims=True) for j in range(7)]
+    sums[3] = jnp.where(lower, sums[3], sums[6])
+    tail = jnp.concatenate(sums[:6] + [jnp.zeros((2, LANES), f32)], 0)
+
+    @pl.loop(0, blocks, unroll=blocks)
     def _(a):
         rows = out[a, tokens + half :].astype(f32)
         out[a, tokens + half :] = jnp.concatenate([rows[:8], tail], 0).astype(out.dtype)

time: 79.9 us -> 78.9 us (0.987)
  Pallas kernels: 15 us -> 14.1 us
    pallas_call x1, Pallas kernels: 9.82 us -> 8.87 us  [per_device(): pl.pallas_call(resident, out_shape=jax.ShapeDtypeStruct((blocks, rows_out...]
where the time goes in v6:
time: 78.9 us; the launch traced here: 78.5 us
  waiting for transfers between devices  48 us (61%)
  starting transfers between devices  15.2 us (19%)
  Pallas kernels  14.1 us (18%)
  between operations  0.8 us (1%)
    all_to_all x1, waiting for transfers between devices, per_device(): owned_chunk = lax.all_to_all(packed, 'seq', 0, 0, tiled=True)  29 us
    all_to_all x1, waiting for transfers between devices, per_device(): back = lax.all_to_all(returned, 'seq', 0, 0, tiled=True)  19 us
    pallas_call x1, Pallas kernels, per_device(): pl.pallas_call(resident, out_shape=jax.ShapeDtypeStruct((blocks, rows_out...  8.87 us
    all_to_all x1, starting transfers between devices, per_device(): owned_chunk = lax.all_to_all(packed, 'seq', 0, 0, tiled=True)  8.46 us
    all_to_all x1, starting transfers between devices, per_device(): back = lax.all_to_all(returned, 'seq', 0, 0, tiled=True)  6.72 us
    pallas_call x1, Pallas kernels, per_device(): pl.pallas_call(pack_kernel, out_shape=jax.ShapeDtypeStruct((blocks, rows_...  2.55 us
    pallas_call x1, Pallas kernels, per_device(): pl.pallas_call(finish_kernel, out_shape=[jax.ShapeDtypeStruct(shape, bf16...  1.91 us
  transfers between devices with their start and end apart: 2, of which 2 were waited for; matrix products, arithmetic and copies ran while one was open for 1% of the time, Pallas kernels for 1%

profile of v6, /device:TPU:0, one launch (start us, length us, event | category | flops | bytes accessed | tf_op | source)
XLA Modules:
  0.0 78.5 jit_solution(10334993482420281399)
XLA Ops:
  0.6 2.6 %pack.1 = bf16[16,320,128]{2,1,0:T(8,128)(2,1)} custom-call(bf16[128,1024]{1,0:T(8,128)(2,1)} %one.3, bf16[128,1024]{1,0:T(8,128)(2,1)} %two.3, bf16[128,1024]{1,0:T(8,128)(2,1)} %value.3, bf16[128,1024]{1,0:T(8,128)(2,1)} %filt.1, bf16[128,1024]{1,0:T(8,128)(2,1)} %grad.3), custom_call_target="tpu_custom_call" | custom-call | tf_op jit(solution)/shard_map/pack/pallas_call | solution.py:596
  3.2 0.0 copy-start.6
  3.2 0.0 slice-start
  3.2 0.0 slice-start.1
  3.2 0.0 copy-start.5
  3.2 8.5 %all-to-all-start = ((bf16[16,320,128]{2,1,0:T(8,128)(2,1)}), bf16[16,320,128]{2,1,0:T(8,128)(2,1)S(1)}, u32[]{:S(2)}, u32[]{:S(2)}) async-start(bf16[16,320,128]{2,1,0:T(8,128)(2,1)} %pack.1), calls=%async_computation | async-start | bytes 2621440 | tf_op jit(solution)/shard_map/all_to_all | solution.py:619
  11.7 0.0 copy-done.6
  11.7 0.1 concatenate.20
  11.8 0.0 slice-done
  11.8 0.1 concatenate.22
  11.9 0.0 slice-done.1
  11.9 0.1 concatenate.19
  12.0 0.0 copy-done.5
  12.1 0.1 fusion.3.refs_1_
  12.1 29.0 %all-to-all-done.refs_0_ = bf16[16,320,128]{2,1,0:T(8,128)(2,1)S(1)} async-done(((bf16[16,320,128]{2,1,0:T(8,128)(2,1)}), bf16[16,320,128]{2,1,0:T(8,128)(2,1)S(1)}, u32[]{:S(2)}, u32[]{:S(2)}) %all-to-all-start) | async-done | bytes 1310752 | tf_op jit(solution)/shard_map/all_to_all | solution.py:619
  41.2 8.9 %owner.1.after = bf16[16,208,128]{2,1,0:T(8,128)(2,1)} custom-call(bf16[16,320,128]{2,1,0:T(8,128)(2,1)S(1)} %all-to-all-done.refs_0_, f32[8,128]{1,0:T(8,128)S(1)} %fusion.3.refs_1_, bf16[2,17,128,512]{3,2,1,0:T(8,128)(2,1)} %constant.47.clone.refs_2_), custom_call_target="tpu_custom_call" | custom-call | tf_op jit(solution)/shard_map/owner/pallas_call | solution.py:631
  50.0 0.0 copy-start
  50.0 0.0 copy-start.1
  50.1 0.0 copy-start.2
  50.1 0.0 copy-start.4
  50.1 6.7 %all-to-all-start.1 = ((bf16[16,208,128]{2,1,0:T(8,128)(2,1)}), bf16[16,208,128]{2,1,0:T(8,128)(2,1)S(1)}, u32[]{:S(2)}, u32[]{:S(2)}) async-start(bf16[16,208,128]{2,1,0:T(8,128)(2,1)} %owner.1.after), calls=%async_computation.1 | async-start | bytes 1703936 | tf_op jit(solution)/shard_map/all_to_all | solution.py:678
  56.8 0.0 copy-done
  56.8 0.0 copy-done.1
  56.8 0.0 copy-done.2
  56.8 0.0 copy-done.4
  56.8 0.0 copy-start.3
  56.9 0.8 gates.1
  57.6 19.0 %all-to-all-done.1.back = bf16[16,208,128]{2,1,0:T(8,128)(2,1)S(1)} async-done(((bf16[16,208,128]{2,1,0:T(8,128)(2,1)}), bf16[16,208,128]{2,1,0:T(8,128)(2,1)S(1)}, u32[]{:S(2)}, u32[]{:S(2)}) %all-to-all-start.1) | async-done | bytes 852000 | tf_op jit(solution)/shard_map/all_to_all | solution.py:678
  76.6 0.0 copy-done.3
  76.6 1.9 %finish.1 = (bf16[128,1024]{1,0:T(8,128)(2,1)}, bf16[128,1024]{1,0:T(8,128)(2,1)}, bf16[128,1024]{1,0:T(8,128)(2,1)}, bf16[128,1024]{1,0:T(8,128)(2,1)}, f32[128...) custom-call(f32[3,128,1024]{2,1,0:T(8,128)S(1)} %gates.1, bf16[128,1024]{1,0:T(8,128)(2,1)S(1)} %copy-done.3, ...), custom_call_target="tpu_custom_call" | custom-call | tf_op jit(solution)/shard_map/finish/pallas_call | solution.py:693
  (3 shorter events, 0.1 us)
Async XLA Ops:
  3.2 8.5 %copy-start.6 = (f32[1024]{0:T(1024)S(1)}, f32[1024]{0:T(1024)}, u32[]{:S(2)}) copy-start(f32[1024]{0:T(1024)} %param.15) | copy-start | bytes 12292
  3.2 8.6 %slice-start = ((f32[3,3,1024]{2,1,0:T(4,128)}), f32[1,3,1024]{2,1,0:T(4,128)S(1)}, s32[]{:S(2)}) async-start(f32[3,3,1024]{2,1,0:T(4,128)} %weights.3), calls=%async_computation.2 | async-start | bytes 32768 | tf_op jit(solution)/shard_map/slice | solution.py:616
  3.2 8.7 %slice-start.1 = ((f32[3,3,1024]{2,1,0:T(4,128)}), f32[2,3,1024]{2,1,0:T(4,128)S(1)}, s32[]{:S(2)}) async-start(f32[3,3,1024]{2,1,0:T(4,128)} %weights.3), calls=%async_computation.3 | async-start | bytes 65536 | tf_op jit(solution)/shard_map/slice | solution.py:615
  3.2 8.8 %copy-start.5 = (f32[3,16,64]{2,0,1:T(4,128)S(1)}, f32[3,16,64]{2,0,1:T(4,128)}, u32[]{:S(2)}) copy-start(f32[3,16,64]{2,0,1:T(4,128)} %constant.42.clone.1) | copy-start | bytes 36868
  3.2 37.9 %all-to-all-start = ((bf16[16,320,128]{2,1,0:T(8,128)(2,1)}), bf16[16,320,128]{2,1,0:T(8,128)(2,1)S(1)}, u32[]{:S(2)}, u32[]{:S(2)}) async-start(bf16[16,320,128]{2,1,0:T(8,128)(2,1)} %pack.1), calls=%async_computation | async-start | bytes 2621440 | tf_op jit(solution)/shard_map/all_to_all | solution.py:619
  50.0 6.8 %copy-start = (bf16[128,1024]{1,0:T(8,128)(2,1)S(1)}, bf16[128,1024]{1,0:T(8,128)(2,1)}, u32[]{:S(2)}) copy-start(bf16[128,1024]{1,0:T(8,128)(2,1)} %one.3) | copy-start | bytes 786436
  50.0 6.8 %copy-start.1 = (bf16[128,1024]{1,0:T(8,128)(2,1)S(1)}, bf16[128,1024]{1,0:T(8,128)(2,1)}, u32[]{:S(2)}) copy-start(bf16[128,1024]{1,0:T(8,128)(2,1)} %two.3) | copy-start | bytes 786436
  50.1 6.8 %copy-start.2 = (bf16[128,1024]{1,0:T(8,128)(2,1)S(1)}, bf16[128,1024]{1,0:T(8,128)(2,1)}, u32[]{:S(2)}) copy-start(bf16[128,1024]{1,0:T(8,128)(2,1)} %value.3) | copy-start | bytes 786436
  50.1 6.8 %copy-start.4 = (f32[3,3,1024]{2,1,0:T(4,128)S(1)}, f32[3,3,1024]{2,1,0:T(4,128)}, u32[]{:S(2)}) copy-start(f32[3,3,1024]{2,1,0:T(4,128)} %weights.3) | copy-start | bytes 110596
  50.1 26.5 %all-to-all-start.1 = ((bf16[16,208,128]{2,1,0:T(8,128)(2,1)}), bf16[16,208,128]{2,1,0:T(8,128)(2,1)S(1)}, u32[]{:S(2)}, u32[]{:S(2)}) async-start(bf16[16,208,128]{2,1,0:T(8,128)(2,1)} %owner.1.after), calls=%async_computation.1 | async-start | bytes 1703936 | tf_op jit(solution)/shard_map/all_to_all | solution.py:678
  56.8 19.8 %copy-start.3 = (bf16[128,1024]{1,0:T(8,128)(2,1)S(1)}, bf16[128,1024]{1,0:T(8,128)(2,1)}, u32[]{:S(2)}) copy-start(bf16[128,1024]{1,0:T(8,128)(2,1)} %grad.3) | copy-start | bytes 786436

commit v7 on v6

--- a/solution.py
+++ b/solution.py
@@ -271,7 +271,7 @@
 
 def resident_kernel(
     blocks, chunk, weights, tables_hbm, out,
-    tables, high_ref, low_ref, zh_ref, zl_ref, spec_ref,
+    tables, raw_ref, zh_ref, zl_ref, spec_ref,
     s1_ref, s2_ref, c1_ref, c2_ref, ug_ref, lg_ref, gf_ref, acc_ref, sems,
 ):
     tokens = tables.shape[2]
@@ -317,9 +317,7 @@
         acc_ref[6] += folded(ug * halves_swapped(ug))
 
     def put(k, row, cols, values):
-        high = values.astype(bf16)
-        high_ref[k, pl.ds(row, 16), cols] = high
-        low_ref[k, pl.ds(row, 16), cols] = (values - high.astype(f32)).astype(bf16)
+        raw_ref[k, pl.ds(row, 16), cols] = values
 
     left, right = slice(0, LANES), slice(LANES, 2 * LANES)
 
@@ -360,7 +358,9 @@
     sign = jnp.where(lax.broadcasted_iota(jnp.int32, (1, LANES), 1) < HALF, 1.0, -1.0)
 
     def into_products(k, slot):
-        spectral = apply(0, k, high_ref[k], low_ref[k])
+        raw = raw_ref[k]
+        coarse = raw.astype(bf16)
+        spectral = apply(0, k, coarse, (raw - coarse.astype(f32)).astype(bf16))
         ur, ui = spectral[:tokens, :LANES], spectral[tokens:, :LANES]
         hr, hi = spectral[:tokens, LANES:], spectral[tokens:, LANES:] * sign
         vr, vi = halves_swapped(ur), halves_swapped(ui)
@@ -635,8 +635,7 @@
             out_specs=VMEM,
             scratch_shapes=[
                 pltpu.VMEM((2, blocks + 1, tokens, 2 * size), bf16),
-                pltpu.VMEM((blocks + 1, size, 2 * LANES), bf16),
-                pltpu.VMEM((blocks + 1, size, 2 * LANES), bf16),
+                pltpu.VMEM((blocks + 1, size, 2 * LANES), f32),
                 pltpu.VMEM((2 * group, size, 2 * LANES), bf16),
                 pltpu.VMEM((2 * group, size, 2 * LANES), bf16),
                 pltpu.VMEM((blocks + 1, size, 2 * LANES), f32),

time: 78.9 us -> 78.6 us (level)
  no operation moved by 1% of the time
where the time goes in v7:
time: 78.6 us; the launch traced here: 78.2 us
  waiting for transfers between devices  48 us (61%)
  starting transfers between devices  15.2 us (19%)
  Pallas kernels  13.8 us (18%)
  between operations  0.8 us (1%)
    all_to_all x1, waiting for transfers between devices, per_device(): owned_chunk = lax.all_to_all(packed, 'seq', 0, 0, tiled=True)  29 us
    all_to_all x1, waiting for transfers between devices, per_device(): back = lax.all_to_all(returned, 'seq', 0, 0, tiled=True)  19 us
    pallas_call x1, Pallas kernels, per_device(): pl.pallas_call(resident, out_shape=jax.ShapeDtypeStruct((blocks, rows_out...  8.58 us
    all_to_all x1, starting transfers between devices, per_device(): owned_chunk = lax.all_to_all(packed, 'seq', 0, 0, tiled=True)  8.46 us
    all_to_all x1, starting transfers between devices, per_device(): back = lax.all_to_all(returned, 'seq', 0, 0, tiled=True)  6.71 us
    pallas_call x1, Pallas kernels, per_device(): pl.pallas_call(pack_kernel, out_shape=jax.ShapeDtypeStruct((blocks, rows_...  2.55 us
    pallas_call x1, Pallas kernels, per_device(): pl.pallas_call(finish_kernel, out_shape=[jax.ShapeDtypeStruct(shape, bf16...  1.91 us
  transfers between devices with their start and end apart: 2, of which 2 were waited for; matrix products, arithmetic and copies ran while one was open for 1% of the time, Pallas kernels for 1%

profile of v7, /device:TPU:0, one launch (start us, length us, event | category | flops | bytes accessed | tf_op | source)
XLA Modules:
  0.0 78.2 jit_solution(11884970176197081453)
XLA Ops:
  0.6 2.6 %pack.1 = bf16[16,320,128]{2,1,0:T(8,128)(2,1)} custom-call(bf16[128,1024]{1,0:T(8,128)(2,1)} %one.3, bf16[128,1024]{1,0:T(8,128)(2,1)} %two.3, bf16[128,1024]{1,0:T(8,128)(2,1)} %value.3, bf16[128,1024]{1,0:T(8,128)(2,1)} %filt.1, bf16[128,1024]{1,0:T(8,128)(2,1)} %grad.3), custom_call_target="tpu_custom_call" | custom-call | tf_op jit(solution)/shard_map/pack/pallas_call | solution.py:596
  3.2 0.0 copy-start.6
  3.2 0.0 slice-start
  3.2 0.0 slice-start.1
  3.2 0.0 copy-start.5
  3.2 8.5 %all-to-all-start = ((bf16[16,320,128]{2,1,0:T(8,128)(2,1)}), bf16[16,320,128]{2,1,0:T(8,128)(2,1)S(1)}, u32[]{:S(2)}, u32[]{:S(2)}) async-start(bf16[16,320,128]{2,1,0:T(8,128)(2,1)} %pack.1), calls=%async_computation | async-start | bytes 2621440 | tf_op jit(solution)/shard_map/all_to_all | solution.py:619
  11.7 0.0 copy-done.6
  11.7 0.1 concatenate.20
  11.8 0.0 slice-done
  11.8 0.1 concatenate.22
  11.9 0.0 slice-done.1
  11.9 0.1 concatenate.19
  12.0 0.0 copy-done.5
  12.1 0.1 fusion.3.refs_1_
  12.1 29.0 %all-to-all-done.refs_0_ = bf16[16,320,128]{2,1,0:T(8,128)(2,1)S(1)} async-done(((bf16[16,320,128]{2,1,0:T(8,128)(2,1)}), bf16[16,320,128]{2,1,0:T(8,128)(2,1)S(1)}, u32[]{:S(2)}, u32[]{:S(2)}) %all-to-all-start) | async-done | bytes 1310752 | tf_op jit(solution)/shard_map/all_to_all | solution.py:619
  41.2 8.6 %owner.1.after = bf16[16,208,128]{2,1,0:T(8,128)(2,1)} custom-call(bf16[16,320,128]{2,1,0:T(8,128)(2,1)S(1)} %all-to-all-done.refs_0_, f32[8,128]{1,0:T(8,128)S(1)} %fusion.3.refs_1_, bf16[2,17,128,512]{3,2,1,0:T(8,128)(2,1)} %constant.47.clone.refs_2_), custom_call_target="tpu_custom_call" | custom-call | tf_op jit(solution)/shard_map/owner/pallas_call | solution.py:631
  49.7 0.0 copy-start
  49.8 0.0 copy-start.1
  49.8 0.0 copy-start.2
  49.8 0.0 copy-start.4
  49.8 6.7 %all-to-all-start.1 = ((bf16[16,208,128]{2,1,0:T(8,128)(2,1)}), bf16[16,208,128]{2,1,0:T(8,128)(2,1)S(1)}, u32[]{:S(2)}, u32[]{:S(2)}) async-start(bf16[16,208,128]{2,1,0:T(8,128)(2,1)} %owner.1.after), calls=%async_computation.1 | async-start | bytes 1703936 | tf_op jit(solution)/shard_map/all_to_all | solution.py:677
  56.5 0.0 copy-done
  56.5 0.0 copy-done.1
  56.5 0.0 copy-done.2
  56.5 0.0 copy-done.4
  56.6 0.0 copy-start.3
  56.6 0.8 gates.1
  57.3 19.0 %all-to-all-done.1.back = bf16[16,208,128]{2,1,0:T(8,128)(2,1)S(1)} async-done(((bf16[16,208,128]{2,1,0:T(8,128)(2,1)}), bf16[16,208,128]{2,1,0:T(8,128)(2,1)S(1)}, u32[]{:S(2)}, u32[]{:S(2)}) %all-to-all-start.1) | async-done | bytes 852000 | tf_op jit(solution)/shard_map/all_to_all | solution.py:677
  76.3 0.0 copy-done.3
  76.3 1.9 %finish.1 = (bf16[128,1024]{1,0:T(8,128)(2,1)}, bf16[128,1024]{1,0:T(8,128)(2,1)}, bf16[128,1024]{1,0:T(8,128)(2,1)}, bf16[128,1024]{1,0:T(8,128)(2,1)}, f32[128...) custom-call(f32[3,128,1024]{2,1,0:T(8,128)S(1)} %gates.1, bf16[128,1024]{1,0:T(8,128)(2,1)S(1)} %copy-done.3, ...), custom_call_target="tpu_custom_call" | custom-call | tf_op jit(solution)/shard_map/finish/pallas_call | solution.py:692
  (3 shorter events, 0.1 us)
Async XLA Ops:
  3.2 8.5 %copy-start.6 = (f32[1024]{0:T(1024)S(1)}, f32[1024]{0:T(1024)}, u32[]{:S(2)}) copy-start(f32[1024]{0:T(1024)} %param.15) | copy-start | bytes 12292
  3.2 8.6 %slice-start = ((f32[3,3,1024]{2,1,0:T(4,128)}), f32[1,3,1024]{2,1,0:T(4,128)S(1)}, s32[]{:S(2)}) async-start(f32[3,3,1024]{2,1,0:T(4,128)} %weights.3), calls=%async_computation.2 | async-start | bytes 32768 | tf_op jit(solution)/shard_map/slice | solution.py:616
  3.2 8.7 %slice-start.1 = ((f32[3,3,1024]{2,1,0:T(4,128)}), f32[2,3,1024]{2,1,0:T(4,128)S(1)}, s32[]{:S(2)}) async-start(f32[3,3,1024]{2,1,0:T(4,128)} %weights.3), calls=%async_computation.3 | async-start | bytes 65536 | tf_op jit(solution)/shard_map/slice | solution.py:615
  3.2 8.8 %copy-start.5 = (f32[3,16,64]{2,0,1:T(4,128)S(1)}, f32[3,16,64]{2,0,1:T(4,128)}, u32[]{:S(2)}) copy-start(f32[3,16,64]{2,0,1:T(4,128)} %constant.42.clone.1) | copy-start | bytes 36868
  3.2 37.9 %all-to-all-start = ((bf16[16,320,128]{2,1,0:T(8,128)(2,1)}), bf16[16,320,128]{2,1,0:T(8,128)(2,1)S(1)}, u32[]{:S(2)}, u32[]{:S(2)}) async-start(bf16[16,320,128]{2,1,0:T(8,128)(2,1)} %pack.1), calls=%async_computation | async-start | bytes 2621440 | tf_op jit(solution)/shard_map/all_to_all | solution.py:619
  49.7 6.8 %copy-start = (bf16[128,1024]{1,0:T(8,128)(2,1)S(1)}, bf16[128,1024]{1,0:T(8,128)(2,1)}, u32[]{:S(2)}) copy-start(bf16[128,1024]{1,0:T(8,128)(2,1)} %one.3) | copy-start | bytes 786436
  49.8 6.8 %copy-start.1 = (bf16[128,1024]{1,0:T(8,128)(2,1)S(1)}, bf16[128,1024]{1,0:T(8,128)(2,1)}, u32[]{:S(2)}) copy-start(bf16[128,1024]{1,0:T(8,128)(2,1)} %two.3) | copy-start | bytes 786436
  49.8 6.8 %copy-start.2 = (bf16[128,1024]{1,0:T(8,128)(2,1)S(1)}, bf16[128,1024]{1,0:T(8,128)(2,1)}, u32[]{:S(2)}) copy-start(bf16[128,1024]{1,0:T(8,128)(2,1)} %value.3) | copy-start | bytes 786436
  49.8 6.8 %copy-start.4 = (f32[3,3,1024]{2,1,0:T(4,128)S(1)}, f32[3,3,1024]{2,1,0:T(4,128)}, u32[]{:S(2)}) copy-start(f32[3,3,1024]{2,1,0:T(4,128)} %weights.3) | copy-start | bytes 110596
  49.8 26.5 %all-to-all-start.1 = ((bf16[16,208,128]{2,1,0:T(8,128)(2,1)}), bf16[16,208,128]{2,1,0:T(8,128)(2,1)S(1)}, u32[]{:S(2)}, u32[]{:S(2)}) async-start(bf16[16,208,128]{2,1,0:T(8,128)(2,1)} %owner.1.after), calls=%async_computation.1 | async-start | bytes 1703936 | tf_op jit(solution)/shard_map/all_to_all | solution.py:677
  56.6 19.8 %copy-start.3 = (bf16[128,1024]{1,0:T(8,128)(2,1)S(1)}, bf16[128,1024]{1,0:T(8,128)(2,1)}, u32[]{:S(2)}) copy-start(bf16[128,1024]{1,0:T(8,128)(2,1)} %grad.3) | copy-start | bytes 786436

commit v8 on v7

--- a/solution.py
+++ b/solution.py
@@ -327,7 +327,8 @@
         spectrum = padded_dft([ug_ref[a, pl.ds(at, 16)].astype(f32) for a in range(blocks)])
         for k, (real, imag) in enumerate(spectrum):
             put(k, at, left, real)
-            put(k, tokens + at, left, jnp.zeros_like(real) if imag is None else imag)
+            if imag is not None:
+                put(k, tokens + at, left, imag)
 
     @pl.loop(0, half // 16, unroll=2)
     def _(r):
@@ -338,7 +339,8 @@
         )
         for k, pair in enumerate(spectrum):
             for place, part in enumerate(pair):
-                part = jnp.zeros_like(pair[0]) if part is None else part
+                if part is None:
+                    continue
                 turned = halves_swapped(part)
                 put(k, place * tokens + at, right, jnp.where(low, part, turned))
                 put(k, place * tokens + half + at, right, jnp.where(low, turned, part))
@@ -349,16 +351,22 @@
             [pair, jnp.concatenate([-pair[:, tokens:], pair[:, :tokens]], 1)], 0
         )
 
+    def is_real(k):
+        return isinstance(k, int) and k in (0, blocks)
+
     def apply(table, k, high, rest):
-        first = whole_map(table, k, 0)
+        rows = tokens if is_real(k) and table == 1 else size
+        depth = high.shape[0]
+        first = whole_map(table, k, 0)[:rows, :depth]
         total = jnp.dot(first, high, preferred_element_type=f32)
-        total = total + jnp.dot(whole_map(table, k, size), high, preferred_element_type=f32)
+        second = whole_map(table, k, size)[:rows, :depth]
+        total = total + jnp.dot(second, high, preferred_element_type=f32)
         return total + jnp.dot(first, rest, preferred_element_type=f32)
 
     sign = jnp.where(lax.broadcasted_iota(jnp.int32, (1, LANES), 1) < HALF, 1.0, -1.0)
 
     def into_products(k, slot):
-        raw = raw_ref[k]
+        raw = raw_ref[k, :tokens] if is_real(k) else raw_ref[k]
         coarse = raw.astype(bf16)
         spectral = apply(0, k, coarse, (raw - coarse.astype(f32)).astype(bf16))
         ur, ui = spectral[:tokens, :LANES], spectral[tokens:, :LANES]
@@ -376,7 +384,8 @@
             zl_ref[slot, rows, cols] = (values - high.astype(f32)).astype(bf16)
 
     def out_of_products(k, slot):
-        spec_ref[k] = apply(1, k, zh_ref[slot], zl_ref[slot])
+        values = apply(1, k, zh_ref[slot], zl_ref[slot])
+        spec_ref[k, : values.shape[0]] = values
 
     copies[0].wait()
 
@@ -387,9 +396,8 @@
         into_products(j, j)
     copies[1].wait()
 
-    @pl.loop(1, whole)
-    def _(i):
-        now = lax.rem(i, 2) * group
+    for i in range(1, whole):
+        now = i % 2 * group
         for j in range(group):
             out_of_products((i - 1) * group + j, group - now + j)
         for j in range(group):

time: 78.6 us -> 78.2 us (level)
  no operation moved by 1% of the time
where the time goes in v8:
time: 78.2 us; the launch traced here: 77.8 us
  waiting for transfers between devices  48 us (61%)
  starting transfers between devices  15.2 us (19%)
  Pallas kernels  13.4 us (17%)
  between operations  0.8 us (1%)
    all_to_all x1, waiting for transfers between devices, per_device(): owned_chunk = lax.all_to_all(packed, 'seq', 0, 0, tiled=True)  29 us
    all_to_all x1, waiting for transfers between devices, per_device(): back = lax.all_to_all(returned, 'seq', 0, 0, tiled=True)  19 us
    all_to_all x1, starting transfers between devices, per_device(): owned_chunk = lax.all_to_all(packed, 'seq', 0, 0, tiled=True)  8.46 us
    pallas_call x1, Pallas kernels, per_device(): pl.pallas_call(resident, out_shape=jax.ShapeDtypeStruct((blocks, rows_out...  8.14 us
    all_to_all x1, starting transfers between devices, per_device(): back = lax.all_to_all(returned, 'seq', 0, 0, tiled=True)  6.71 us
    pallas_call x1, Pallas kernels, per_device(): pl.pallas_call(pack_kernel, out_shape=jax.ShapeDtypeStruct((blocks, rows_...  2.55 us
    pallas_call x1, Pallas kernels, per_device(): pl.pallas_call(finish_kernel, out_shape=[jax.ShapeDtypeStruct(shape, bf16...  1.91 us
  transfers between devices with their start and end apart: 2, of which 2 were waited for; matrix products, arithmetic and copies ran while one was open for 1% of the time, Pallas kernels for 1%

profile of v8, /device:TPU:0, one launch (start us, length us, event | category | flops | bytes accessed | tf_op | source)
XLA Modules:
  0.0 77.8 jit_solution(14617988216493079600)
XLA Ops:
  0.6 2.6 %pack.1 = bf16[16,320,128]{2,1,0:T(8,128)(2,1)} custom-call(bf16[128,1024]{1,0:T(8,128)(2,1)} %one.3, bf16[128,1024]{1,0:T(8,128)(2,1)} %two.3, bf16[128,1024]{1,0:T(8,128)(2,1)} %value.3, bf16[128,1024]{1,0:T(8,128)(2,1)} %filt.1, bf16[128,1024]{1,0:T(8,128)(2,1)} %grad.3), custom_call_target="tpu_custom_call" | custom-call | tf_op jit(solution)/shard_map/pack/pallas_call | solution.py:604
  3.2 0.0 copy-start.6
  3.2 0.0 slice-start
  3.2 0.0 slice-start.1
  3.2 0.0 copy-start.5
  3.2 8.5 %all-to-all-start = ((bf16[16,320,128]{2,1,0:T(8,128)(2,1)}), bf16[16,320,128]{2,1,0:T(8,128)(2,1)S(1)}, u32[]{:S(2)}, u32[]{:S(2)}) async-start(bf16[16,320,128]{2,1,0:T(8,128)(2,1)} %pack.1), calls=%async_computation | async-start | bytes 2621440 | tf_op jit(solution)/shard_map/all_to_all | solution.py:627
  11.7 0.0 copy-done.6
  11.7 0.1 concatenate.20
  11.8 0.0 slice-done
  11.8 0.1 concatenate.22
  11.9 0.0 slice-done.1
  11.9 0.1 concatenate.19
  12.0 0.0 copy-done.5
  12.1 0.1 fusion.3.refs_1_
  12.1 29.0 %all-to-all-done.refs_0_ = bf16[16,320,128]{2,1,0:T(8,128)(2,1)S(1)} async-done(((bf16[16,320,128]{2,1,0:T(8,128)(2,1)}), bf16[16,320,128]{2,1,0:T(8,128)(2,1)S(1)}, u32[]{:S(2)}, u32[]{:S(2)}) %all-to-all-start) | async-done | bytes 1310752 | tf_op jit(solution)/shard_map/all_to_all | solution.py:627
  41.2 8.1 %owner.1.after = bf16[16,208,128]{2,1,0:T(8,128)(2,1)} custom-call(bf16[16,320,128]{2,1,0:T(8,128)(2,1)S(1)} %all-to-all-done.refs_0_, f32[8,128]{1,0:T(8,128)S(1)} %fusion.3.refs_1_, bf16[2,17,128,512]{3,2,1,0:T(8,128)(2,1)} %constant.47.clone.refs_2_), custom_call_target="tpu_custom_call" | custom-call | tf_op jit(solution)/shard_map/owner/pallas_call | solution.py:639
  49.3 0.0 copy-start
  49.3 0.0 copy-start.1
  49.3 0.0 copy-start.2
  49.3 0.0 copy-start.4
  49.3 6.7 %all-to-all-start.1 = ((bf16[16,208,128]{2,1,0:T(8,128)(2,1)}), bf16[16,208,128]{2,1,0:T(8,128)(2,1)S(1)}, u32[]{:S(2)}, u32[]{:S(2)}) async-start(bf16[16,208,128]{2,1,0:T(8,128)(2,1)} %owner.1.after), calls=%async_computation.1 | async-start | bytes 1703936 | tf_op jit(solution)/shard_map/all_to_all | solution.py:685
  56.1 0.0 copy-done
  56.1 0.0 copy-done.1
  56.1 0.0 copy-done.2
  56.1 0.0 copy-done.4
  56.1 0.0 copy-start.3
  56.1 0.8 gates.1
  56.9 19.0 %all-to-all-done.1.back = bf16[16,208,128]{2,1,0:T(8,128)(2,1)S(1)} async-done(((bf16[16,208,128]{2,1,0:T(8,128)(2,1)}), bf16[16,208,128]{2,1,0:T(8,128)(2,1)S(1)}, u32[]{:S(2)}, u32[]{:S(2)}) %all-to-all-start.1) | async-done | bytes 852000 | tf_op jit(solution)/shard_map/all_to_all | solution.py:685
  75.9 0.0 copy-done.3
  75.9 1.9 %finish.1 = (bf16[128,1024]{1,0:T(8,128)(2,1)}, bf16[128,1024]{1,0:T(8,128)(2,1)}, bf16[128,1024]{1,0:T(8,128)(2,1)}, bf16[128,1024]{1,0:T(8,128)(2,1)}, f32[128...) custom-call(f32[3,128,1024]{2,1,0:T(8,128)S(1)} %gates.1, bf16[128,1024]{1,0:T(8,128)(2,1)S(1)} %copy-done.3, ...), custom_call_target="tpu_custom_call" | custom-call | tf_op jit(solution)/shard_map/finish/pallas_call | solution.py:700
  (3 shorter events, 0.1 us)
Async XLA Ops:
  3.2 8.5 %copy-start.6 = (f32[1024]{0:T(1024)S(1)}, f32[1024]{0:T(1024)}, u32[]{:S(2)}) copy-start(f32[1024]{0:T(1024)} %param.15) | copy-start | bytes 12292
  3.2 8.6 %slice-start = ((f32[3,3,1024]{2,1,0:T(4,128)}), f32[1,3,1024]{2,1,0:T(4,128)S(1)}, s32[]{:S(2)}) async-start(f32[3,3,1024]{2,1,0:T(4,128)} %weights.3), calls=%async_computation.2 | async-start | bytes 32768 | tf_op jit(solution)/shard_map/slice | solution.py:624
  3.2 8.7 %slice-start.1 = ((f32[3,3,1024]{2,1,0:T(4,128)}), f32[2,3,1024]{2,1,0:T(4,128)S(1)}, s32[]{:S(2)}) async-start(f32[3,3,1024]{2,1,0:T(4,128)} %weights.3), calls=%async_computation.3 | async-start | bytes 65536 | tf_op jit(solution)/shard_map/slice | solution.py:623
  3.2 8.8 %copy-start.5 = (f32[3,16,64]{2,0,1:T(4,128)S(1)}, f32[3,16,64]{2,0,1:T(4,128)}, u32[]{:S(2)}) copy-start(f32[3,16,64]{2,0,1:T(4,128)} %constant.42.clone.1) | copy-start | bytes 36868
  3.2 37.9 %all-to-all-start = ((bf16[16,320,128]{2,1,0:T(8,128)(2,1)}), bf16[16,320,128]{2,1,0:T(8,128)(2,1)S(1)}, u32[]{:S(2)}, u32[]{:S(2)}) async-start(bf16[16,320,128]{2,1,0:T(8,128)(2,1)} %pack.1), calls=%async_computation | async-start | bytes 2621440 | tf_op jit(solution)/shard_map/all_to_all | solution.py:627
  49.3 6.8 %copy-start = (bf16[128,1024]{1,0:T(8,128)(2,1)S(1)}, bf16[128,1024]{1,0:T(8,128)(2,1)}, u32[]{:S(2)}) copy-start(bf16[128,1024]{1,0:T(8,128)(2,1)} %one.3) | copy-start | bytes 786436
  49.3 6.8 %copy-start.1 = (bf16[128,1024]{1,0:T(8,128)(2,1)S(1)}, bf16[128,1024]{1,0:T(8,128)(2,1)}, u32[]{:S(2)}) copy-start(bf16[128,1024]{1,0:T(8,128)(2,1)} %two.3) | copy-start | bytes 786436
  49.3 6.8 %copy-start.2 = (bf16[128,1024]{1,0:T(8,128)(2,1)S(1)}, bf16[128,1024]{1,0:T(8,128)(2,1)}, u32[]{:S(2)}) copy-start(bf16[128,1024]{1,0:T(8,128)(2,1)} %value.3) | copy-start | bytes 786436
  49.3 6.8 %copy-start.4 = (f32[3,3,1024]{2,1,0:T(4,128)S(1)}, f32[3,3,1024]{2,1,0:T(4,128)}, u32[]{:S(2)}) copy-start(f32[3,3,1024]{2,1,0:T(4,128)} %weights.3) | copy-start | bytes 110596
  49.3 26.5 %all-to-all-start.1 = ((bf16[16,208,128]{2,1,0:T(8,128)(2,1)}), bf16[16,208,128]{2,1,0:T(8,128)(2,1)S(1)}, u32[]{:S(2)}, u32[]{:S(2)}) async-start(bf16[16,208,128]{2,1,0:T(8,128)(2,1)} %owner.1.after), calls=%async_computation.1 | async-start | bytes 1703936 | tf_op jit(solution)/shard_map/all_to_all | solution.py:685
  56.1 19.8 %copy-start.3 = (bf16[128,1024]{1,0:T(8,128)(2,1)S(1)}, bf16[128,1024]{1,0:T(8,128)(2,1)}, u32[]{:S(2)}) copy-start(bf16[128,1024]{1,0:T(8,128)(2,1)} %grad.3) | copy-start | bytes 786436
